TPU v7x, 128 devices: a whole 4x4x4 slice. The times are simulated.
128 devices in a mesh: batch: 128 (over y, x, z, core).
Axes of the slice: x: 4, y: 4, z: 4, core: 2. Of those that a mesh axis runs over, the one named last changes fastest.
Arguments:
- features: bfloat16 [128, 16, 8, 16, 256], P('batch'), may hold values from -6 to 6
- timesteps: int32 [1024], replicated, may hold values from 0 to 255
- embedding: float32 [256, 1024], replicated, may hold values from -6 to 6
- first_gain: float32 [256], replicated, may hold values from 0.1 to 1.9
- first_shift: float32 [256], replicated, may hold values from -3 to 3
- first_kernel: bfloat16 [3, 3, 256, 256], replicated, may hold values from -0.125 to 0.125
- first_bias: float32 [256], replicated, may hold values from -3 to 3
- time_dense: bfloat16 [1024, 256], replicated, may hold values from -0.1875 to 0.1875
- second_gain: float32 [256], replicated, may hold values from 0.1 to 1.9
- second_shift: float32 [256], replicated, may hold values from -3 to 3
- second_kernel: bfloat16 [3, 3, 256, 256], replicated, may hold values from -0.125 to 0.125
- second_bias: float32 [256], replicated, may hold values from -3 to 3
- mixer_gain: float32 [256], replicated, may hold values from 0.1 to 1.9
- mixer_shift: float32 [256], replicated, may hold values from -3 to 3
- project_in: bfloat16 [256, 768], replicated, may hold values from -0.375 to 0.375
- query_bias: float32 [256], replicated, may hold values from -2 to 2
- value_bias: float32 [256], replicated, may hold values from -2 to 2
- project_out: bfloat16 [256, 256], replicated, may hold values from -1.5 to 1.5
- output_bias: float32 [256], replicated, may hold values from -3 to 3
- cotangent: bfloat16 [128, 16, 8, 16, 256], P('batch'), may hold values from -6 to 6
Outputs:
- result: bfloat16 [128, 16, 8, 16, 256], P('batch')
- input_grad: float32 [128, 16, 8, 16, 256], P('batch')
- embedding_grad: float32 [256, 1024], replicated
- first_gain_grad: float32 [256], replicated
- first_shift_grad: float32 [256], replicated
- first_kernel_grad: float32 [3, 3, 256, 256], replicated
- first_bias_grad: float32 [256], replicated
- time_dense_grad: float32 [1024, 256], replicated
- second_gain_grad: float32 [256], replicated
- second_shift_grad: float32 [256], replicated
- second_kernel_grad: float32 [3, 3, 256, 256], replicated
- second_bias_grad: float32 [256], replicated
- mixer_gain_grad: float32 [256], replicated
- mixer_shift_grad: float32 [256], replicated
- project_in_grad: float32 [256, 768], replicated
- query_bias_grad: float32 [256], replicated
- value_bias_grad: float32 [256], replicated
- project_out_grad: float32 [256, 256], replicated
- output_bias_grad: float32 [256], replicated
All inputs are finite; a program needn't handle non-finite values.
Results may differ from a plain program's by a relative error of at most 0.017.
Values may be sent and summed in bfloat16 or wider, within the bound.
No kernel may reach another device: no remote copies, remote signals or barrier semaphores. Data moves between devices by JAX's collectives and lax.ppermute only.
A program may use at most 128 MiB of HBM per device.

v0:
```python
import jax
import jax.numpy as jnp
from jax import lax
from jax.experimental import pallas as pl
from jax.experimental.pallas import tpu as pltpu
from jax.sharding import PartitionSpec as P

BF = jnp.bfloat16
F32 = jnp.float32
C = 256
SIDE = 16
POS = 256
GROUPS = 32
LANES = 128
EPSILON = 1e-05
OWN = 8
PAD = POS + 2 * SIDE
COUNT = float(POS * C // GROUPS)

G1, S1, B1, G2, S2, B2, G3, S3, BQ, BV, BO = range(11)
MU1, RS1, MU2, RS2 = range(4)


def mm(a, b):
    return jnp.dot(a, b, preferred_element_type=F32)


def mm_nt(a, b):
    return lax.dot_general(a, b, (((1,), (1,)), ((), ())), preferred_element_type=F32)


def mm_tn(a, b):
    return lax.dot_general(a, b, (((0,), (0,)), ((), ())), preferred_element_type=F32)


def group_total(s):
    lane = lax.broadcasted_iota(jnp.int32, s.shape, 1)
    for bit in (1, 2, 4):
        s = s + jnp.where((lane & bit) == 0, pltpu.roll(s, C - bit, 1), pltpu.roll(s, bit, 1))
    return s


def statistics(total, squares):
    mu = group_total(total) * (1.0 / COUNT)
    var = group_total(squares) * (1.0 / COUNT) - mu * mu
    return mu, lax.rsqrt(var + EPSILON)


def logistic(z):
    return 0.5 * jnp.tanh(0.5 * z) + 0.5


def row_sum(v):
    return jnp.sum(v, axis=0, keepdims=True)


def row(ref, index):
    return ref[pl.ds(index, 1), :]


def put_shifted(ref, slot, wide, left_first):
    column = lax.broadcasted_iota(jnp.int32, wide.shape, 0) & (SIDE - 1)
    from_left = jnp.where(column == 0, 0.0, pltpu.roll(wide, 1, 0)).astype(BF)
    from_right = jnp.where(column == SIDE - 1, 0.0, pltpu.roll(wide, POS - 1, 0)).astype(BF)
    first, last = (from_left, from_right) if left_first else (from_right, from_left)
    ref[slot, SIDE : SIDE + POS, 0:C] = first
    ref[slot, SIDE : SIDE + POS, C : 2 * C] = wide.astype(BF)
    ref[slot, SIDE : SIDE + POS, 2 * C : 3 * C] = last


def clear_edges(ref):
    edge = jnp.zeros((SIDE, 3 * C), BF)
    for slot in range(OWN // 2):
        ref[slot, 0:SIDE, :] = edge
        ref[slot, SIDE + POS : PAD, :] = edge


def conv(ref, slot, weights, backward):
    starts = [SIDE * (2 - a) if backward else SIDE * a for a in range(3)]
    window = jnp.concatenate(
        [
            ref[pl.ds(slot, 2), start : start + POS, :].reshape(2 * POS, 3 * C)
            for start in starts
        ],
        axis=1,
    )
    return mm(window, weights[...]).reshape(2, POS, C)


def put_block(out, index, value):
    out[index * C : (index + 1) * C, :] = value.astype(BF)


def weight_taps(out, first, a, transposed, shifted):
    rows = slice(SIDE * (2 - a), SIDE * (2 - a) + POS)
    for b in range(3):
        right = jnp.concatenate(
            [
                ref[:, rows, b * C : (b + 1) * C].reshape(OWN // 2 * POS, C)
                for ref in shifted
            ]
        )
        put_block(out, first + a * 3 + b, mm(transposed[...], right))


def columns_of(place):
    return slice(place * POS, (place + 1) * POS)


def overlapped(ahead, after):
    def both(pair):
        for index in range(2):
            ahead(2 * pair + index, pair % 2, pair // 2 * 2 + index)

    both(0)
    for pair in range(1, OWN // 2):
        both(pair)
        after(2 * pair - 2, (pair - 1) % 2, (pair - 1) // 2 * 2)
    after(OWN - 2, 1, OWN // 2 - 2)


def kernel_body(
    place, steps, own_x, own_g, got, emb, dense, k1, k2, w_in, w_out,
    v0, v1, v2, v3, v4, v5, v6, v7, v8, v9, v10,
    result, result_send, input_own, input_send, grads_keep, grads_send,
    x_ref, g_ref, at_ref, et_ref, a3_even, a3_odd, e3_even, e3_odd, c1_ref, d1_ref, d2_ref, r_ref,
    nt_ref, ot_ref, dq_ref, dn_ref, z_ref, dr_ref, res_ref, send_ref, k1_ref, k2_ref, k1t, k2t,
    emb_ref, dense_ref, steps_grad, grads, small, sums, st, coef, added, vec, sem,
):
    core = lax.rem(place[0], 2)
    base = place[0] * OWN
    mine = pl.ds(core * OWN, OWN)
    a3 = (a3_even, a3_odd)
    e3 = (e3_even, e3_odd)
    copies = [
        pltpu.make_async_copy(own_x.at[mine], x_ref.at[:, core], sem.at[0]),
        pltpu.make_async_copy(got.at[0:OWN], x_ref.at[:, 1 - core], sem.at[1]),
        pltpu.make_async_copy(k1, k1_ref, sem.at[2]),
        pltpu.make_async_copy(dense, dense_ref, sem.at[4]),
        pltpu.make_async_copy(k2, k2_ref, sem.at[5]),
        pltpu.make_async_copy(own_g.at[mine], g_ref.at[:, core], sem.at[6]),
        pltpu.make_async_copy(got.at[OWN:], g_ref.at[:, 1 - core], sem.at[7]),
    ]
    for copy in copies:
        copy.start()
    eights = []
    for m in range(OWN):
        first = pl.multiple_of(steps[base + m] // 8 * 8, 8)
        copy = pltpu.make_async_copy(emb.at[pl.ds(first, 8)], emb_ref.at[m], sem.at[16 + m])
        copy.start()
        eights.append(copy)
    for index, ref in enumerate((v0, v1, v2, v3, v4, v5, v6, v7, v8, v9, v10)):
        vec[index : index + 1, :] = ref[...].reshape(1, C)
    for ref in a3 + e3:
        clear_edges(ref)
    small[...] = jnp.zeros_like(small)
    grads[BLOCKS * C + 16 :, :] = jnp.zeros((ROWS - BLOCKS * C - 16, C), BF)
    steps_grad[...] = jnp.zeros_like(steps_grad)

    def param(index):
        return vec[index : index + 1, :]

    def load_x(m):
        return x_ref[m].reshape(POS, C).astype(F32)

    def load_g(m):
        return g_ref[m].reshape(POS, C)

    def put_sums(m, first, second):
        sums[0, pl.ds(m, 1), :] = row_sum(first)
        sums[1, pl.ds(m, 1), :] = row_sum(second)

    copies[0].wait()
    copies[1].wait()

    for m in range(OWN):
        x = load_x(m)
        put_sums(m, x, x * x)

    mu, rs = statistics(sums[0], sums[1])
    st[MU1] = mu
    st[RS1] = rs
    coef[0] = rs * param(G1)

    for copy in copies[2:4] + eights:
        copy.wait()
    u = jnp.concatenate(
        [emb_ref[m, pl.ds(lax.rem(steps[base + m], 8), 1), :] for m in range(OWN)], axis=0
    )
    w = (u * logistic(u)).astype(BF)
    added[...] = mm(w, dense_ref[...]) + param(B1)

    def transpose_block(to, from_, index):
        at = columns_of(index)
        to[at, :] = from_[at, :].T

    def activate(from_, deriv, transposed, shifted, mu, shift):
        def ahead(m, parity, slot):
            z = (from_(m) - row(mu, m)) * row(coef.at[0], m) + shift
            s = logistic(z)
            a = z * s
            deriv[m] = (s + a * (1.0 - s)).astype(BF)
            transposed[:, columns_of(slot + parity * (OWN // 2))] = a.astype(BF).T
            put_shifted(shifted[parity], slot, a, True)

        return ahead

    def first_conv(m, parity, slot):
        both = conv(a3[parity], slot, k1_ref, False)
        for index in range(2):
            transpose_block(k1t, k1_ref, m + index)
            c1 = both[index] + row(added, m + index)
            c1_ref[m + index] = c1
            put_sums(m + index, c1, c1 * c1)

    overlapped(activate(load_x, d1_ref, at_ref, a3, st.at[MU1], param(S1)), first_conv)
    transpose_block(k1t, k1_ref, 8)

    mu, rs = statistics(sums[0], sums[1])
    st[MU2] = mu
    st[RS2] = rs
    coef[0] = rs * param(G2)
    copies[4].wait()

    def second_conv(m, parity, slot):
        both = conv(e3[parity], slot, k2_ref, False)
        for index in range(2):
            transpose_block(k2t, k2_ref, m + index)
            r = load_x(m + index) + both[index] + param(B2)
            r_ref[m + index] = r
            put_sums(m + index, r, r * r)

    overlapped(
        activate(lambda m: c1_ref[m], d2_ref, et_ref, e3, st.at[MU2], param(S2)), second_conv
    )
    transpose_block(k2t, k2_ref, 8)

    mu, rs = statistics(sums[0], sums[1])
    coef[0] = mu
    coef[1] = rs
    coef[2] = rs * param(G3)
    copies[5].wait()
    copies[6].wait()

    def two(rows):
        return [rows[0:POS], rows[POS : 2 * POS]]

    def attention(pair):
        maps = [2 * pair, 2 * pair + 1]
        scale = C ** (-0.5)
        r = [r_ref[m] for m in maps]
        t = [v - row(coef.at[0], m) for v, m in zip(r, maps)]
        n = [(v * row(coef.at[2], m) + param(S3)).astype(BF) for v, m in zip(t, maps)]
        for v, m in zip(n, maps):
            nt_ref[:, columns_of(m)] = v.T
        joined = two(mm(jnp.concatenate(n), w_in[...]))
        q = [
            ((v[:, 0:C] + param(BQ)).astype(BF).astype(F32) * scale).astype(BF) for v in joined
        ]
        k = [v[:, C : 2 * C].astype(BF) for v in joined]
        v = [b[:, 2 * C :] + param(BV) for b in joined]
        v = [b.astype(BF) for b in v]
        g = [load_g(m) for m in maps]
        do = two(mm_nt(jnp.concatenate(g), w_out[...]).astype(BF))
        scores = [mm_nt(a, b) for a, b in zip(k, q)]
        dp = [mm_nt(a, b) for a, b in zip(v, do)]
        e = [jnp.exp(a - jnp.max(a, axis=0, keepdims=True)) for a in scores]
        p = [a * (1.0 / jnp.sum(a, axis=0, keepdims=True)) for a in e]
        low = [a.astype(BF) for a in p]
        ds = [(a * (b - row_sum(a * b))).astype(BF) for a, b in zip(p, dp)]
        o = [mm_tn(a, b).astype(BF) for a, b in zip(low, v)]
        dv = [mm(a, b).astype(BF) for a, b in zip(low, do)]
        dk = [mm(a, b).astype(BF) for a, b in zip(ds, q)]
        dq = [(mm_tn(a, b) * scale).astype(BF) for a, b in zip(ds, k)]
        for m, a in zip(maps, o):
            ot_ref[:, columns_of(m)] = a.T
        for m, a, b in zip(maps, r, two(mm(jnp.concatenate(o), w_out[...]))):
            res = a + b + param(BO)
            res_ref[m] = res.astype(BF).reshape(2, HALF, C)
        together = [jnp.concatenate(parts, axis=1) for parts in zip(dq, dk, dv)]
        dn = two(mm_nt(jnp.concatenate(together), w_in[...]))
        for m, a, b, c in zip(maps, together, dn, t):
            dq_ref[m] = a
            dn_ref[m] = b
            put_sums(m, b, b * (c * row(coef.at[1], m)))
        for index, parts in enumerate((dq, dv, g)):
            total = row_sum(parts[0].astype(F32)) + row_sum(parts[1].astype(F32))
            small[index : index + 1, :] += total

    for pair in range(OWN // 2):
        attention(pair)

    give = [
        pltpu.make_async_copy(res_ref.at[:, core], result.at[mine], sem.at[8]),
        pltpu.make_async_copy(res_ref.at[:, 1 - core], result_send, sem.at[9]),
    ]
    for copy in give:
        copy.start()

    def finish_norm(rs, gain, at):
        small[at : at + 1, :] = row_sum(sums[1])
        small[at + 1 : at + 2, :] = row_sum(sums[0])
        coef[2] = rs * gain
        coef[3] = rs * rs * group_total(sums[1] * gain) * (1.0 / COUNT)
        coef[4] = rs * group_total(sums[0] * gain) * (1.0 / COUNT)

    def norm_grad(g, t, m):
        return g * row(coef.at[2], m) - t * row(coef.at[3], m) - row(coef.at[4], m)

    finish_norm(coef[1], param(G3), 3)

    def mixer_back(m, parity, slot):
        dr = load_g(m).astype(F32) + norm_grad(dn_ref[m], r_ref[m] - row(coef.at[0], m), m)
        dr_ref[m] = dr
        low = dr.astype(BF).astype(F32)
        small[5:6, :] += row_sum(low)
        put_shifted(a3[parity], slot, low, False)

    def second_back(m, parity, slot):
        both = conv(a3[parity], slot, k2t, True)
        for index in range(2):
            at = m + index
            g = both[index] * d2_ref[at].astype(F32)
            z_ref[at] = g
            put_sums(at, g, g * ((c1_ref[at] - row(st.at[MU2], at)) * row(st.at[RS2], at)))

    overlapped(mixer_back, second_back)

    for a in range(3):
        weight_taps(grads, 0, a, et_ref, a3)
    flat = dq_ref[...].reshape(OWN * POS, 3 * C)
    for part in range(3):
        put_block(grads, 9 + part, mm(nt_ref[...], flat[:, part * C : (part + 1) * C]))
    put_block(grads, 12, mm(ot_ref[...], g_ref[...].reshape(OWN * POS, C)))

    def leave_low(to):
        return pltpu.make_async_copy(grads.at[0:PART], to, sem.at[12])

    def leave_high(at, rows, index):
        def to(ref):
            source = grads.at[PART + at : PART + at + rows]
            return pltpu.make_async_copy(source, ref.at[at : at + rows], sem.at[index])

        return to

    @pl.when(core == 0)
    def _():
        leave_low(grads_keep).start()

    @pl.when(core == 1)
    def _():
        leave_low(grads_send).start()

    finish_norm(st[RS2], param(G2), 6)

    def hidden_back(m, parity, slot):
        t = c1_ref[m] - row(st.at[MU2], m)
        low = norm_grad(z_ref[m], t, m).astype(BF).astype(F32)
        total = row_sum(low)
        small[8:9, :] += total
        where = pl.ds(steps[base + m], 1)
        steps_grad[where, :] = steps_grad[where, :] + total
        put_shifted(e3[parity], slot, low, False)

    def centered(m):
        return load_x(m) - row(st.at[MU1], m)

    def first_back(m, parity, slot):
        both = conv(e3[parity], slot, k1t, True)
        for index in range(2):
            at = m + index
            g = both[index] * d1_ref[at].astype(F32)
            dn_ref[at] = g
            put_sums(at, g, g * (centered(at) * row(st.at[RS1], at)))

    overlapped(hidden_back, first_back)
    put_block(grads, 22, steps_grad[...])
    finish_norm(st[RS1], param(G1), 9)
    grads[BLOCKS * C : BLOCKS * C + 16, :] = small[...].astype(BF)
    away = pl.ds((1 - core) * HALF, HALF)

    def input_back(m):
        r_ref[m] = dr_ref[m] + norm_grad(dn_ref[m], centered(m), m)
        send_ref[m] = r_ref[m, away, :].astype(BF)

    for a in range(2):
        for index in range(3):
            input_back(3 * a + index)
        weight_taps(grads, 13, a, at_ref, e3)

    pieces = [leave_high(0, 7 * C, 14), leave_high(7 * C, PART - 7 * C, 15)]

    @pl.when(core == 0)
    def _():
        pieces[0](grads_send).start()

    @pl.when(core == 1)
    def _():
        pieces[0](grads_keep).start()

    input_back(6)
    input_back(7)
    give += [
        pltpu.make_async_copy(r_ref.at[:, pl.ds(core * HALF, HALF)], input_own.at[mine], sem.at[10]),
        pltpu.make_async_copy(send_ref, input_send, sem.at[11]),
    ]
    for copy in give[2:]:
        copy.start()
    weight_taps(grads, 13, 2, at_ref, e3)

    @pl.when(core == 0)
    def _():
        last = pieces[1](grads_send)
        last.start()
        leave_low(grads_keep).wait()
        pieces[0](grads_send).wait()
        last.wait()

    @pl.when(core == 1)
    def _():
        last = pieces[1](grads_keep)
        last.start()
        leave_low(grads_send).wait()
        pieces[0](grads_keep).wait()
        last.wait()

    for copy in give:
        copy.wait()


def shape(*dims, kind=F32):
    return jax.ShapeDtypeStruct(dims, kind)


SMEM = pl.BlockSpec(memory_space=pltpu.SMEM)
VMEM = pl.BlockSpec(memory_space=pltpu.VMEM)
ANY = pl.BlockSpec(memory_space=pl.ANY)
FULL = 60 * 1024 * 1024
ALL = 62 * 1024 * 1024
MOST = 40 * 1024 * 1024
LEAST = 16 * 1024 * 1024
HALF = POS // 2
MAP = (OWN, POS, C)
BANDS = (OWN, 2, HALF, C)
TRIPLE = (OWN // 2, PAD, 3 * C)
WIDE = (C, OWN * POS)
BLOCKS = 23
VECTORS = 11
PEERS = 64
EIGHT = 8
EIGHTH = 384
EVENLY = (1, 2, 4, 7, 3, 5, 6)
PART = EIGHT * EIGHTH
ROWS = 2 * PART


def run(place, steps, own_x, own_g, got, emb, dense, k1, k2, w_in, w_out, vectors):
    return pl.pallas_call(
        kernel_body,
        in_specs=[SMEM, SMEM] + [ANY] * 7 + [VMEM] * 13,
        out_specs=[ANY] * 6,
        out_shape=[
            shape(2 * OWN, HALF, C, kind=BF),
            shape(OWN, HALF, C, kind=BF),
            shape(2 * OWN, HALF, C),
            shape(OWN, HALF, C, kind=BF),
            shape(PART, C, kind=BF),
            shape(PART, C, kind=BF),
        ],
        scratch_shapes=[
            pltpu.VMEM(BANDS, BF),
            pltpu.VMEM(BANDS, BF),
            pltpu.VMEM(WIDE, BF),
            pltpu.VMEM(WIDE, BF),
            pltpu.VMEM(TRIPLE, BF),
            pltpu.VMEM(TRIPLE, BF),
            pltpu.VMEM(TRIPLE, BF),
            pltpu.VMEM(TRIPLE, BF),
            pltpu.VMEM(MAP, F32),
            pltpu.VMEM(MAP, BF),
            pltpu.VMEM(MAP, BF),
            pltpu.VMEM(MAP, F32),
            pltpu.VMEM(WIDE, BF),
            pltpu.VMEM(WIDE, BF),
            pltpu.VMEM((OWN, POS, 3 * C), BF),
            pltpu.VMEM(MAP, F32),
            pltpu.VMEM(MAP, F32),
            pltpu.VMEM(MAP, F32),
            pltpu.VMEM(BANDS, BF),
            pltpu.VMEM((OWN, HALF, C), BF),
            pltpu.VMEM((9 * C, C), BF),
            pltpu.VMEM((9 * C, C), BF),
            pltpu.VMEM((9 * C, C), BF),
            pltpu.VMEM((9 * C, C), BF),
            pltpu.VMEM((OWN, 8, 4 * C), F32),
            pltpu.VMEM((4 * C, C), BF),
            pltpu.VMEM((C, C), F32),
            pltpu.VMEM((ROWS, C), BF),
            pltpu.VMEM((16, C), F32),
            pltpu.VMEM((2, OWN, C), F32),
            pltpu.VMEM((4, OWN, C), F32),
            pltpu.VMEM((5, OWN, C), F32),
            pltpu.VMEM((OWN, C), F32),
            pltpu.VMEM((16, C), F32),
            pltpu.SemaphoreType.DMA((16 + OWN,)),
        ],
        compiler_params=pltpu.CompilerParams(vmem_limit_bytes=FULL),
        cost_estimate=pl.CostEstimate(
            flops=20 * 10**9, bytes_accessed=20 * 10**6, transcendentals=3 * 10**6
        ),
    )(place, steps, own_x, own_g, got, emb, dense, k1, k2, w_in, w_out, *vectors)


def swap(block):
    count = lax.axis_size("batch")
    return lax.ppermute(block, "batch", [(i, i ^ 1) for i in range(count)])


def join_body(place, mine_r, mine_i, got_r, got_i, out_r, out_i, wide_i, sem):
    there = pl.ds((1 - lax.rem(place[0], 2)) * OWN, OWN)
    first = pltpu.make_async_copy(got_r, out_r.at[there], sem.at[0])
    first.start()
    wide_i[...] = got_i[...].astype(F32)
    second = pltpu.make_async_copy(wide_i, out_i.at[there], sem.at[1])
    second.start()
    first.wait()
    second.wait()


def join(place, mine_r, mine_i, got_r, got_i):
    return pl.pallas_call(
        join_body,
        in_specs=[SMEM, ANY, ANY, ANY, VMEM],
        out_specs=[ANY, ANY],
        out_shape=[shape(*mine_r.shape, kind=BF), shape(*mine_i.shape)],
        input_output_aliases={1: 0, 2: 1},
        scratch_shapes=[pltpu.VMEM((OWN, HALF, C), F32), pltpu.SemaphoreType.DMA((2,))],
        compiler_params=pltpu.CompilerParams(vmem_limit_bytes=LEAST),
        cost_estimate=pl.CostEstimate(flops=0, bytes_accessed=4 * 10**6, transcendentals=0),
    )(place, mine_r, mine_i, got_r, got_i)


def load_body(x, out, sem):
    copy = pltpu.make_async_copy(x, out, sem)
    copy.start()
    copy.wait()


def nearby(x):
    return pl.pallas_call(
        load_body,
        in_specs=[ANY],
        out_specs=VMEM,
        out_shape=shape(*x.shape, kind=x.dtype),
        scratch_shapes=[pltpu.SemaphoreType.DMA],
        compiler_params=pltpu.CompilerParams(vmem_limit_bytes=LEAST),
        cost_estimate=pl.CostEstimate(flops=0, bytes_accessed=2 * 10**6, transcendentals=0),
    )(x)


def wide(ref):
    return ref[...].astype(F32)


def eighth_of(index):
    return pl.ds(pl.multiple_of(index * EIGHTH, EIGHTH), EIGHTH)


def add_body(piece, mine, other, *outs):
    for mask in range(EIGHT):
        at = eighth_of(piece[0] ^ mask)
        total = mine[at, :].astype(F32) + other[at, :].astype(F32)
        outs[mask][...] = total.astype(BF)


def eight_body(*refs):
    total = wide(refs[0])
    for ref in refs[1:EIGHT]:
        total = total + wide(ref)
    low = total.astype(BF)
    for index, out in enumerate(refs[EIGHT:]):
        out[...] = low[index * (EIGHTH // 2) : (index + 1) * (EIGHTH // 2), :]


def two_body(mine, got, out):
    out[...] = (wide(mine) + wide(got)).astype(BF)


def last_body(mine_a, got_a, mine_b, got_b, out):
    out[0 : EIGHTH // 2, :] = (wide(mine_a) + wide(got_a)).astype(BF)
    out[EIGHTH // 2 :, :] = (wide(mine_b) + wide(got_b)).astype(BF)


def place_body(piece, *refs):
    for index, mask in enumerate((0,) + EVENLY):
        refs[EIGHT][eighth_of(piece[0] ^ mask), :] = refs[index][...]


def small_call(kernel, rows, count, *operands):
    scalars = [SMEM] if operands[0].ndim == 1 else []
    return pl.pallas_call(
        kernel,
        in_specs=scalars + [VMEM] * (len(operands) - len(scalars)),
        out_specs=[VMEM] * count,
        out_shape=[shape(rows, C, kind=BF)] * count,
        compiler_params=pltpu.CompilerParams(vmem_limit_bytes=LEAST),
        cost_estimate=pl.CostEstimate(flops=10**6, bytes_accessed=10**6, transcendentals=0),
    )(*operands)


def shifts(core):
    return [core, core, 1 - core]


def lines(index):
    return [
        (index // 2 // 4**axis + 3 * shift) % 4 for axis, shift in enumerate(shifts(index % 2))
    ]


def device_at(places, core):
    chip = sum(
        (place + shift) % 4 * 4**axis
        for axis, (place, shift) in enumerate(zip(places, shifts(core)))
    )
    return 2 * chip + core


def exchange(block, moved):
    pairs = [
        (index, device_at(moved(lines(index)), index % 2)) for index in range(2 * PEERS)
    ]
    return lax.ppermute(block, "batch", pairs)


def near(mask):
    return lambda places: [p ^ (mask >> axis & 1) for axis, p in enumerate(places)]


def far(axis):
    return lambda places: [3 - p if at == axis else p for at, p in enumerate(places)]


def all_sum(keep, other, device, meanwhile, afterwards):
    bits = [(place + 1) // 2 % 2 for place in lines(device)]
    piece = (bits[0] + 2 * bits[1] + 4 * bits[2]).reshape(1).astype(jnp.int32)
    sends = small_call(add_body, EIGHTH, EIGHT, piece, nearby(keep), other)
    arrived = meanwhile(sends[0])
    early, late = EVENLY[:3], EVENLY[3:]
    got = [exchange(sends[mask], near(mask)) for mask in early]
    held, arrived = lax.optimization_barrier(([sends[mask] for mask in late], arrived))
    got += [exchange(block, near(mask)) for block, mask in zip(held, late)]
    first, beside = lax.optimization_barrier((sends[0], afterwards(arrived)))
    a, b = small_call(eight_body, EIGHTH // 2, 2, first, *got)
    for step in range(2):
        a, b = (
            small_call(two_body, EIGHTH // 2, 1, part, exchange(part, far((step + first) % 3)))[0]
            for first, part in enumerate((a, b))
        )
    whole = small_call(
        last_body, EIGHTH, 1, a, exchange(a, far(2)), b, exchange(b, far(0))
    )[0]
    got = [exchange(whole, near(mask)) for mask in EVENLY]
    mine = small_call(place_body, PART, 1, piece, whole, *got)[0]
    return mine, swap(mine), beside


def write_half(high, part, emb, dense, outs, stage, wide_stage, table, emb_ref, dense_ref, sem):
    second_grad, in_grad, out_grad, first_grad, dense_grad, emb_grad = outs
    if high:
        places = [out_grad] + [first_grad.at[index] for index in range(9)]
        fetch = [
            pltpu.make_async_copy(emb, emb_ref, sem.at[18]),
            pltpu.make_async_copy(dense, dense_ref, sem.at[19]),
        ]
        for copy in fetch:
            copy.start()
    else:
        places = [second_grad.at[index] for index in range(9)]
        places += [in_grad.at[:, index * C : (index + 1) * C] for index in range(3)]
    copies = []

    def leave(source, to):
        copy = pltpu.make_async_copy(source, to, sem.at[len(copies)])
        copy.start()
        copies.append(copy)

    for index, to in enumerate(places):
        stage[index] = part[index * C : (index + 1) * C, :].astype(F32)
        leave(stage.at[index], to)
    if high:
        table[...] = part[10 * C : 11 * C, :]
        for copy in fetch:
            copy.wait()
        for index in range(4):
            columns = slice(index * C, (index + 1) * C)
            u = emb_ref[:, columns]
            s = logistic(u)
            active = u * s
            wide_stage[0, index] = mm(active.astype(BF).T, table[...])
            leave(wide_stage.at[0, index], dense_grad.at[columns, :])
            slope = s + active * (1.0 - s)
            wide_stage[1, index] = mm_nt(table[...], dense_ref[columns, :]) * slope
            leave(wide_stage.at[1, index], emb_grad.at[:, columns])
    for copy in copies:
        copy.wait()


def finish_own_body(place, mine, emb, dense, *refs):
    outs, scratch = refs[:6], refs[6:]
    for core in range(2):

        @pl.when(lax.rem(place[0], 2) == core)
        def _():
            write_half(core == 1, mine, emb, dense, outs, *scratch)


def finish_other_body(place, mine, other, emb, dense, *refs):
    outs, vectors, scratch = refs[6:12], refs[12 : 12 + VECTORS], refs[12 + VECTORS :]
    core = lax.rem(place[0], 2)
    at = slice(11 * C, 11 * C + 16)
    rows = jnp.where(core == 1, mine[at, :].astype(F32), other[at, :].astype(F32))
    for index, out in enumerate(vectors):
        out[...] = rows[index : index + 1, :].reshape(C)
    for this in range(2):

        @pl.when(core == this)
        def _():
            write_half(this == 0, other, emb, dense, outs, *scratch)


def finish(place, mine, other, emb, dense):
    dims = [(9, C, C), (C, 3 * C), (C, C), (9, C, C), (4 * C, C), (C, 4 * C)]
    settings = dict(
        scratch_shapes=[
            pltpu.VMEM((12, C, C), F32),
            pltpu.VMEM((2, 4, C, C), F32),
            pltpu.VMEM((C, C), BF),
            pltpu.VMEM((C, 4 * C), F32),
            pltpu.VMEM((4 * C, C), BF),
            pltpu.SemaphoreType.DMA((20,)),
        ],
        compiler_params=pltpu.CompilerParams(vmem_limit_bytes=LEAST),
        cost_estimate=pl.CostEstimate(
            flops=10**8, bytes_accessed=6 * 10**6, transcendentals=10**5
        ),
    )
    outs = pl.pallas_call(
        finish_own_body,
        in_specs=[SMEM, VMEM, ANY, ANY],
        out_specs=[ANY] * 6,
        out_shape=[shape(*d) for d in dims],
        **settings,
    )(place, mine, emb, dense)
    return pl.pallas_call(
        finish_other_body,
        in_specs=[SMEM, VMEM, VMEM, ANY, ANY] + [ANY] * 6,
        out_specs=[ANY] * 6 + [VMEM] * VECTORS,
        out_shape=[shape(*d) for d in dims] + [shape(C)] * VECTORS,
        input_output_aliases={5 + index: index for index in range(6)},
        **settings,
    )(place, mine, other, emb, dense, *outs)


def body(
    features, timesteps, embedding, first_gain, first_shift, first_kernel, first_bias, time_dense,
    second_gain, second_shift, second_kernel, second_bias, mixer_gain, mixer_shift, project_in,
    query_bias, value_bias, project_out, output_bias, cotangent,
):
    device = lax.axis_index("batch")
    own_x = features.reshape(2 * OWN, HALF, C)
    own_g = cotangent.reshape(2 * OWN, HALF, C)
    there = (1 - device % 2) * OWN
    place = device.reshape(1).astype(jnp.int32)
    got = swap(
        jnp.concatenate(
            [
                lax.dynamic_slice_in_dim(own_x, there, OWN),
                lax.dynamic_slice_in_dim(own_g, there, OWN),
            ]
        )
    )
    vectors = (
        first_gain, first_shift, first_bias, second_gain, second_shift, second_bias,
        mixer_gain, mixer_shift, query_bias, value_bias, output_bias,
    )
    result, result_send, input_grad, input_send, keep, send = run(
        place, timesteps, own_x, own_g, got, embedding, time_dense,
        first_kernel.reshape(9 * C, C), second_kernel.reshape(9 * C, C), project_in, project_out,
        vectors,
    )
    def swap_maps(block):
        first, second, _ = lax.optimization_barrier((result_send, input_send, block))
        return swap(first), swap(second)

    def join_maps(arrived):
        return join(place, result, input_grad, *arrived)

    mine, other, (result, input_grad) = all_sum(keep, swap(send), device, swap_maps, join_maps)
    (
        second_kernel_grad, in_grad, out_grad, first_kernel_grad, time_dense_grad, embedding_grad,
        *rows,
    ) = finish(place, mine, other, embedding, time_dense)
    banded = features.shape
    return (
        result.reshape(banded),
        input_grad.reshape(banded),
        embedding_grad,
        rows[9],
        rows[10],
        first_kernel_grad.reshape(3, 3, C, C),
        rows[8],
        time_dense_grad,
        rows[6],
        rows[7],
        second_kernel_grad.reshape(3, 3, C, C),
        rows[5],
        rows[3],
        rows[4],
        in_grad,
        rows[0],
        rows[1],
        out_grad,
        rows[2],
    )


def solution(mesh):
    split = P("batch", None, None, None, None)
    return jax.shard_map(
        body,
        mesh=mesh,
        in_specs=(split,) + (P(),) * 18 + (split,),
        out_specs=(split, split) + (P(),) * 17,
        check_vma=False,
    )
```

profile of v0, /device:TPU:1, one launch (start us, length us, event | category | flops | bytes accessed | tf_op | source)
XLA Modules:
  0.0 106.9 jit_solution(7851120858707864575)
XLA Ops:
  0.7 1.3 %constant_dynamic-slice_fusion = (bf16[8,128,256]{2,1,0:T(8,128)(2,1)S(1)}, bf16[8,128,256]{2,1,0:T(8,128)(2,1)S(1)}) fusion(bf16[16,128,256]{2,1,0:T(8,128)(2,1)} %bitcast.16, s32[]{:T(128)S(6)} %select_n.72, bf16[16,128,256]{2,1,0:T(8,128)(2,1)} %bitcast.14), kind=kLoop, calls=%fused_computation.1 | loop fusion | bytes 2097156 | tf_op jit(solution)/shard_map/dynamic_slice | solution.py:779
  2.1 1.5 %collective-permute-start = (bf16[16,128,256]{2,1,0:T(8,128)(2,1)S(1)}, bf16[16,128,256]{2,1,0:T(8,128)(2,1)S(1)}, u32[]{:S(2)}, u32[]{:S(2)}) collective-permute-start(bf16[16,128,256]{2,1,0:T(8,128)(2,1)S(1)} %pad_maximum_fusion), channel_id=1, source_target_pairs={{0,1},{1,0},{2,3},{3,2},{4,5},{5,4},{6,7},{7,6},{8,9},{9,8},{10,11... | collective-permute-start | bytes 3145736 | tf_op jit(solution)/shard_map/ppermute | solution.py:516
  3.6 2.3 %collective-permute-done.got = bf16[16,128,256]{2,1,0:T(8,128)(2,1)S(1)} collective-permute-done((bf16[16,128,256]{2,1,0:T(8,128)(2,1)S(1)}, bf16[16,128,256]{2,1,0:T(8,128)(2,1)S(1)}, u32[]{:S(2)}, u32[]{:S(2)}) %collective-permute-start) | collective-permute-done | bytes 1048608 | tf_op jit(solution)/shard_map/ppermute | solution.py:516
  6.8 31.6 %shard_map.339 = (bf16[16,128,256]{2,1,0:T(8,128)(2,1)}, bf16[8,128,256]{2,1,0:T(8,128)(2,1)}, f32[16,128,256]{2,1,0:T(8,128)}, bf16[8,128,256]{2,1,0:T(8,128)(2...) custom-call(s32[1]{0:T(128)} %bitcast.1.place, s32[1024]{0:T(1024)} %steps.1, bf16[16,128,256]{2,1,0:T(8,128)(2,1)} %bitcast.15, ...), custom_call_target="tpu_custom_call" | custom-call | flops 20000000000 | bytes 20000000 | tf_op jit(solution)/shard_map/pallas_call | solution.py:458
  39.0 1.4 %copy-done.2 = bf16[3072,256]{1,0:T(8,128)(2,1)S(1)} copy-done((bf16[3072,256]{1,0:T(8,128)(2,1)S(1)}, bf16[3072,256]{1,0:T(8,128)(2,1)}, u32[]{:S(2)}) %copy-start.2) | copy-done | bytes 1572888
  40.5 1.7 %collective-permute-done.1.other = bf16[3072,256]{1,0:T(8,128)(2,1)S(1)} collective-permute-done((bf16[3072,256]{1,0:T(8,128)(2,1)}, bf16[3072,256]{1,0:T(8,128)(2,1)S(1)}, u32[]{:S(2)}, u32[]{:S(2)}) %collective-permute-start.1) | collective-permute-done | bytes 1572896 | tf_op jit(solution)/shard_map/ppermute | solution.py:516
  43.8 3.8 %collective-permute-start.4 = (bf16[384,256]{1,0:T(8,128)(2,1)S(1)}, bf16[384,256]{1,0:T(8,128)(2,1)S(1)}, u32[]{:S(2)}, u32[]{:S(2)}) collective-permute-start(bf16[384,256]{1,0:T(8,128)(2,1)S(1)} %get-tuple-element.91), channel_id=1, source_target_pairs={{0,2},{1,7},{2,0},{3,5},{4,6},{5,3},{6,4},{7,1},{8,10},{9,15},{10,... | collective-permute-start | bytes 589832 | tf_op jit(solution)/shard_map/ppermute | solution.py:633
  47.6 2.5 %collective-permute-start.5 = (bf16[384,256]{1,0:T(8,128)(2,1)S(1)}, bf16[384,256]{1,0:T(8,128)(2,1)S(1)}, u32[]{:S(2)}, u32[]{:S(2)}) collective-permute-start(bf16[384,256]{1,0:T(8,128)(2,1)S(1)} %get-tuple-element.92), channel_id=1, source_target_pairs={{0,8},{1,25},{2,10},{3,27},{4,12},{5,29},{6,14},{7,31},{8,0},{9,17... | collective-permute-start | bytes 589832 | tf_op jit(solution)/shard_map/ppermute | solution.py:633
  50.1 1.3 %collective-permute-start.6 = (bf16[384,256]{1,0:T(8,128)(2,1)S(1)}, bf16[384,256]{1,0:T(8,128)(2,1)S(1)}, u32[]{:S(2)}, u32[]{:S(2)}) collective-permute-start(bf16[384,256]{1,0:T(8,128)(2,1)S(1)} %get-tuple-element.93), channel_id=1, source_target_pairs={{0,96},{1,33},{2,98},{3,35},{4,100},{5,37},{6,102},{7,39},{8,104},... | collective-permute-start | bytes 589832 | tf_op jit(solution)/shard_map/ppermute | solution.py:633
  51.4 1.6 %collective-permute-start.7 = (bf16[384,256]{1,0:T(8,128)(2,1)S(1)}, bf16[384,256]{1,0:T(8,128)(2,1)S(1)}, u32[]{:S(2)}, u32[]{:S(2)}) collective-permute-start(bf16[384,256]{1,0:T(8,128)(2,1)S(1)} %get-tuple-element.94), channel_id=1, source_target_pairs={{0,106},{1,63},{2,104},{3,61},{4,110},{5,59},{6,108},{7,57},{8,98}... | collective-permute-start | bytes 589832 | tf_op jit(solution)/shard_map/ppermute | solution.py:633
  53.0 3.1 %collective-permute-start.8 = (bf16[384,256]{1,0:T(8,128)(2,1)S(1)}, bf16[384,256]{1,0:T(8,128)(2,1)S(1)}, u32[]{:S(2)}, u32[]{:S(2)}) collective-permute-start(bf16[384,256]{1,0:T(8,128)(2,1)S(1)} %get-tuple-element.95), channel_id=1, source_target_pairs={{0,10},{1,31},{2,8},{3,29},{4,14},{5,27},{6,12},{7,25},{8,2},{9,23... | collective-permute-start | bytes 589832 | tf_op jit(solution)/shard_map/ppermute | solution.py:633
  56.1 1.1 collective-permute-start.9
  57.1 1.8 %collective-permute-start.10 = (bf16[384,256]{1,0:T(8,128)(2,1)S(1)}, bf16[384,256]{1,0:T(8,128)(2,1)S(1)}, u32[]{:S(2)}, u32[]{:S(2)}) collective-permute-start(bf16[384,256]{1,0:T(8,128)(2,1)S(1)} %get-tuple-element.97), channel_id=1, source_target_pairs={{0,104},{1,57},{2,106},{3,59},{4,108},{5,61},{6,110},{7,63},{8,96}... | collective-permute-start | bytes 589832 | tf_op jit(solution)/shard_map/ppermute | solution.py:633
  59.0 1.2 %shard_map.342 = (bf16[16,128,256]{2,1,0:T(8,128)(2,1)}, f32[16,128,256]{2,1,0:T(8,128)}) custom-call(s32[1]{0:T(128)} %bitcast.1.place, bf16[16,128,256]{2,1,0:T(8,128)(2,1)} %get-tuple-element.74.mine_r, f32[16,128,256]{2,1,0:T(8,128)} %get-tuple-element.75.mine_i, ...), custom_call_target="tpu_custom_call", output_to_operand_aliasing={{0}: (1, {}), {1}: (2, {})} | custom-call | bytes 4000000 | tf_op jit(solution)/shard_map/pallas_call | solution.py:531
  60.1 1.1 %collective-permute-done.7.refs_4_ = bf16[384,256]{1,0:T(8,128)(2,1)S(1)} collective-permute-done((bf16[384,256]{1,0:T(8,128)(2,1)S(1)}, bf16[384,256]{1,0:T(8,128)(2,1)S(1)}, u32[]{:S(2)}, u32[]{:S(2)}) %collective-permute-start.7) | collective-permute-done | bytes 196640 | tf_op jit(solution)/shard_map/ppermute | solution.py:633
  61.2 1.6 %collective-permute-done.8.refs_5_ = bf16[384,256]{1,0:T(8,128)(2,1)S(1)} collective-permute-done((bf16[384,256]{1,0:T(8,128)(2,1)S(1)}, bf16[384,256]{1,0:T(8,128)(2,1)S(1)}, u32[]{:S(2)}, u32[]{:S(2)}) %collective-permute-start.8) | collective-permute-done | bytes 196640 | tf_op jit(solution)/shard_map/ppermute | solution.py:633
  62.8 3.6 %collective-permute-done.9.refs_6_ = bf16[384,256]{1,0:T(8,128)(2,1)S(1)} collective-permute-done((bf16[384,256]{1,0:T(8,128)(2,1)S(1)}, bf16[384,256]{1,0:T(8,128)(2,1)S(1)}, u32[]{:S(2)}, u32[]{:S(2)}) %collective-permute-start.9) | collective-permute-done | bytes 196640 | tf_op jit(solution)/shard_map/ppermute | solution.py:633
  66.8 3.4 %collective-permute-done.11.got = bf16[192,256]{1,0:T(8,128)(2,1)S(1)} collective-permute-done((bf16[192,256]{1,0:T(8,128)(2,1)S(1)}, bf16[192,256]{1,0:T(8,128)(2,1)S(1)}, u32[]{:S(2)}, u32[]{:S(2)}) %collective-permute-start.11) | collective-permute-done | bytes 98336 | tf_op jit(solution)/shard_map/ppermute | solution.py:633
  70.4 2.0 %collective-permute-start.15 = (bf16[192,256]{1,0:T(8,128)(2,1)S(1)}, bf16[192,256]{1,0:T(8,128)(2,1)S(1)}, u32[]{:S(2)}, u32[]{:S(2)}) collective-permute-start(bf16[192,256]{1,0:T(8,128)(2,1)S(1)} %shard_map.346.mine), channel_id=1, source_target_pairs={{0,32},{1,97},{2,34},{3,99},{4,36},{5,101},{6,38},{7,103},{8,40},{... | collective-permute-start | bytes 294920 | tf_op jit(solution)/shard_map/ppermute | solution.py:633
  72.4 1.4 %collective-permute-done.12.got = bf16[192,256]{1,0:T(8,128)(2,1)S(1)} collective-permute-done((bf16[192,256]{1,0:T(8,128)(2,1)S(1)}, bf16[192,256]{1,0:T(8,128)(2,1)S(1)}, u32[]{:S(2)}, u32[]{:S(2)}) %collective-permute-start.12) | collective-permute-done | bytes 98336 | tf_op jit(solution)/shard_map/ppermute | solution.py:633
  73.8 2.0 %collective-permute-start.13 = (bf16[192,256]{1,0:T(8,128)(2,1)S(1)}, bf16[192,256]{1,0:T(8,128)(2,1)S(1)}, u32[]{:S(2)}, u32[]{:S(2)}) collective-permute-start(bf16[192,256]{1,0:T(8,128)(2,1)S(1)} %shard_map.345.mine_a), channel_id=1, source_target_pairs={{0,32},{1,97},{2,34},{3,99},{4,36},{5,101},{6,38},{7,103},{8,40},{... | collective-permute-start | bytes 294920 | tf_op jit(solution)/shard_map/ppermute | solution.py:633
  76.8 1.7 %collective-permute-done.13.got_a = bf16[192,256]{1,0:T(8,128)(2,1)S(1)} collective-permute-done((bf16[192,256]{1,0:T(8,128)(2,1)S(1)}, bf16[192,256]{1,0:T(8,128)(2,1)S(1)}, u32[]{:S(2)}, u32[]{:S(2)}) %collective-permute-start.13) | collective-permute-done | bytes 98336 | tf_op jit(solution)/shard_map/ppermute | solution.py:633
  80.1 1.6 %collective-permute-start.22 = (bf16[384,256]{1,0:T(8,128)(2,1)S(1)}, bf16[384,256]{1,0:T(8,128)(2,1)S(1)}, u32[]{:S(2)}, u32[]{:S(2)}) collective-permute-start(bf16[384,256]{1,0:T(8,128)(2,1)S(1)} %shard_map.348.refs_0_), channel_id=1, source_target_pairs={{0,98},{1,39},{2,96},{3,37},{4,102},{5,35},{6,100},{7,33},{8,106},... | collective-permute-start | bytes 589832 | tf_op jit(solution)/shard_map/ppermute | solution.py:633
  81.7 3.8 %collective-permute-start.21 = (bf16[384,256]{1,0:T(8,128)(2,1)S(1)}, bf16[384,256]{1,0:T(8,128)(2,1)S(1)}, u32[]{:S(2)}, u32[]{:S(2)}) collective-permute-start(bf16[384,256]{1,0:T(8,128)(2,1)S(1)} %shard_map.348.refs_0_), channel_id=1, source_target_pairs={{0,10},{1,31},{2,8},{3,29},{4,14},{5,27},{6,12},{7,25},{8,2},{9,23... | collective-permute-start | bytes 589832 | tf_op jit(solution)/shard_map/ppermute | solution.py:633
  85.5 1.2 %collective-permute-start.20 = (bf16[384,256]{1,0:T(8,128)(2,1)S(1)}, bf16[384,256]{1,0:T(8,128)(2,1)S(1)}, u32[]{:S(2)}, u32[]{:S(2)}) collective-permute-start(bf16[384,256]{1,0:T(8,128)(2,1)S(1)} %shard_map.348.refs_0_), channel_id=1, source_target_pairs={{0,106},{1,63},{2,104},{3,61},{4,110},{5,59},{6,108},{7,57},{8,98}... | collective-permute-start | bytes 589832 | tf_op jit(solution)/shard_map/ppermute | solution.py:633
  87.7 1.8 %collective-permute-start.18 = (bf16[384,256]{1,0:T(8,128)(2,1)S(1)}, bf16[384,256]{1,0:T(8,128)(2,1)S(1)}, u32[]{:S(2)}, u32[]{:S(2)}) collective-permute-start(bf16[384,256]{1,0:T(8,128)(2,1)S(1)} %shard_map.348.refs_0_), channel_id=1, source_target_pairs={{0,8},{1,25},{2,10},{3,27},{4,12},{5,29},{6,14},{7,31},{8,0},{9,17... | collective-permute-start | bytes 589832 | tf_op jit(solution)/shard_map/ppermute | solution.py:633
  89.5 2.3 %collective-permute-start.17 = (bf16[384,256]{1,0:T(8,128)(2,1)S(1)}, bf16[384,256]{1,0:T(8,128)(2,1)S(1)}, u32[]{:S(2)}, u32[]{:S(2)}) collective-permute-start(bf16[384,256]{1,0:T(8,128)(2,1)S(1)} %shard_map.348.refs_0_), channel_id=1, source_target_pairs={{0,2},{1,7},{2,0},{3,5},{4,6},{5,3},{6,4},{7,1},{8,10},{9,15},{10,... | collective-permute-start | bytes 589832 | tf_op jit(solution)/shard_map/ppermute | solution.py:633
  91.8 2.7 %collective-permute-done.20.refs_4_ = bf16[384,256]{1,0:T(8,128)(2,1)S(1)} collective-permute-done((bf16[384,256]{1,0:T(8,128)(2,1)S(1)}, bf16[384,256]{1,0:T(8,128)(2,1)S(1)}, u32[]{:S(2)}, u32[]{:S(2)}) %collective-permute-start.20) | collective-permute-done | bytes 196640 | tf_op jit(solution)/shard_map/ppermute | solution.py:633
  94.4 2.3 %collective-permute-done.17.refs_1_ = bf16[384,256]{1,0:T(8,128)(2,1)S(1)} collective-permute-done((bf16[384,256]{1,0:T(8,128)(2,1)S(1)}, bf16[384,256]{1,0:T(8,128)(2,1)S(1)}, u32[]{:S(2)}, u32[]{:S(2)}) %collective-permute-start.17) | collective-permute-done | bytes 196640 | tf_op jit(solution)/shard_map/ppermute | solution.py:633
  96.8 4.4 %collective-permute-start.24 = (bf16[3072,256]{1,0:T(8,128)(2,1)S(1)}, bf16[3072,256]{1,0:T(8,128)(2,1)S(1)}, u32[]{:S(2)}, u32[]{:S(2)}) collective-permute-start(bf16[3072,256]{1,0:T(8,128)(2,1)S(1)} %shard_map.349.mine), channel_id=1, source_target_pairs={{0,1},{1,0},{2,3},{3,2},{4,5},{5,4},{6,7},{7,6},{8,9},{9,8},{10,11... | collective-permute-start | bytes 4718600 | tf_op jit(solution)/shard_map/ppermute | solution.py:516
  101.2 2.5 %shard_map.350 = (f32[9,256,256]{2,1,0:T(8,128)}, f32[256,768]{1,0:T(8,128)}, f32[256,256]{1,0:T(8,128)}, f32[9,256,256]{2,1,0:T(8,128)}, f32[1024,256]{1,0:T(8,128)}, /*index=5*/f32[256,1024]{1,0:T(8,128)}) custom-call(s32[1]{0:T(128)} %bitcast.1.place, bf16[3072,256]{1,0:T(8,128)(2,1)S(1)} %shard_map.349.mine, f32[256,1024]{1,0:T(8,128)S(1)} %copy-done, ...), custom_call_target="tpu_custom_call" | custom-call | flops 100000000 | bytes 6000000 | tf_op jit(solution)/shard_map/pallas_call | solution.py:748
  104.3 2.5 %shard_map.351 = (f32[9,256,256]{2,1,0:T(8,128)}, f32[256,768]{1,0:T(8,128)}, f32[256,256]{1,0:T(8,128)}, f32[9,256,256]{2,1,0:T(8,128)}, f32[1024,256]{1,0:T(8,...) custom-call(s32[1]{0:T(128)} %bitcast.1.place, ...), custom_call_target="tpu_custom_call", output_to_operand_aliasing={{0}: (5, {}), {1}: (6, {}), {2}: (7, {}), {3}: (8, {}), {4}... | custom-call | flops 100000000 | bytes 6000000 | tf_op jit(solution)/shard_map/pallas_call | solution.py:755
  (45 shorter events, 8.0 us)
Async XLA Ops:
  2.1 3.8 %collective-permute-start = (bf16[16,128,256]{2,1,0:T(8,128)(2,1)S(1)}, bf16[16,128,256]{2,1,0:T(8,128)(2,1)S(1)}, u32[]{:S(2)}, u32[]{:S(2)}) collective-permute-start(bf16[16,128,256]{2,1,0:T(8,128)(2,1)S(1)} %pad_maximum_fusion), channel_id=1, source_target_pairs={{0,1},{1,0},{2,3},{3,2},{4,5},{5,4},{6,7},{7,6},{8,9},{9,8},{10,11... | collective-permute-start | bytes 3145736 | tf_op jit(solution)/shard_map/ppermute | solution.py:516
  5.9 1.0 copy-start.3
  38.4 3.8 %collective-permute-start.1 = (bf16[3072,256]{1,0:T(8,128)(2,1)}, bf16[3072,256]{1,0:T(8,128)(2,1)S(1)}, u32[]{:S(2)}, u32[]{:S(2)}) collective-permute-start(bf16[3072,256]{1,0:T(8,128)(2,1)} %get-tuple-element.72), channel_id=1, source_target_pairs={{0,1},{1,0},{2,3},{3,2},{4,5},{5,4},{6,7},{7,6},{8,9},{9,8},{10,11... | collective-permute-start | bytes 4718600 | tf_op jit(solution)/shard_map/ppermute | solution.py:516
  39.0 1.4 %copy-start.2 = (bf16[3072,256]{1,0:T(8,128)(2,1)S(1)}, bf16[3072,256]{1,0:T(8,128)(2,1)}, u32[]{:S(2)}) copy-start(bf16[3072,256]{1,0:T(8,128)(2,1)} %get-tuple-element.71.x) | copy-start | bytes 4718596
  42.2 1.0 copy-start.5
  42.2 1.4 %copy-start.4 = (bf16[8,128,256]{2,1,0:T(8,128)(2,1)S(1)}, bf16[8,128,256]{2,1,0:T(8,128)(2,1)}, u32[]{:S(2)}) copy-start(bf16[8,128,256]{2,1,0:T(8,128)(2,1)} %get-tuple-element.83) | copy-start | bytes 1572868
  43.3 8.2 %collective-permute-start.2 = (bf16[8,128,256]{2,1,0:T(8,128)(2,1)S(1)}, bf16[8,128,256]{2,1,0:T(8,128)(2,1)S(1)}, u32[]{:S(2)}, u32[]{:S(2)}) collective-permute-start(bf16[8,128,256]{2,1,0:T(8,128)(2,1)S(1)} %copy-done.5), channel_id=1, source_target_pairs={{0,1},{1,0},{2,3},{3,2},{4,5},{5,4},{6,7},{7,6},{8,9},{9,8},{10,11... | collective-permute-start | bytes 1572872 | tf_op jit(solution)/shard_map/ppermute | solution.py:516
  43.6 7.8 %collective-permute-start.3 = (bf16[8,128,256]{2,1,0:T(8,128)(2,1)S(1)}, bf16[8,128,256]{2,1,0:T(8,128)(2,1)S(1)}, u32[]{:S(2)}, u32[]{:S(2)}) collective-permute-start(bf16[8,128,256]{2,1,0:T(8,128)(2,1)S(1)} %copy-done.4), channel_id=1, source_target_pairs={{0,1},{1,0},{2,3},{3,2},{4,5},{5,4},{6,7},{7,6},{8,9},{9,8},{10,11... | collective-permute-start | bytes 1572872 | tf_op jit(solution)/shard_map/ppermute | solution.py:516
  43.8 12.3 %collective-permute-start.4 = (bf16[384,256]{1,0:T(8,128)(2,1)S(1)}, bf16[384,256]{1,0:T(8,128)(2,1)S(1)}, u32[]{:S(2)}, u32[]{:S(2)}) collective-permute-start(bf16[384,256]{1,0:T(8,128)(2,1)S(1)} %get-tuple-element.91), channel_id=1, source_target_pairs={{0,2},{1,7},{2,0},{3,5},{4,6},{5,3},{6,4},{7,1},{8,10},{9,15},{10,... | collective-permute-start | bytes 589832 | tf_op jit(solution)/shard_map/ppermute | solution.py:633
  47.6 9.6 %collective-permute-start.5 = (bf16[384,256]{1,0:T(8,128)(2,1)S(1)}, bf16[384,256]{1,0:T(8,128)(2,1)S(1)}, u32[]{:S(2)}, u32[]{:S(2)}) collective-permute-start(bf16[384,256]{1,0:T(8,128)(2,1)S(1)} %get-tuple-element.92), channel_id=1, source_target_pairs={{0,8},{1,25},{2,10},{3,27},{4,12},{5,29},{6,14},{7,31},{8,0},{9,17... | collective-permute-start | bytes 589832 | tf_op jit(solution)/shard_map/ppermute | solution.py:633
  50.1 10.0 %collective-permute-start.6 = (bf16[384,256]{1,0:T(8,128)(2,1)S(1)}, bf16[384,256]{1,0:T(8,128)(2,1)S(1)}, u32[]{:S(2)}, u32[]{:S(2)}) collective-permute-start(bf16[384,256]{1,0:T(8,128)(2,1)S(1)} %get-tuple-element.93), channel_id=1, source_target_pairs={{0,96},{1,33},{2,98},{3,35},{4,100},{5,37},{6,102},{7,39},{8,104},... | collective-permute-start | bytes 589832 | tf_op jit(solution)/shard_map/ppermute | solution.py:633
  51.4 9.8 %collective-permute-start.7 = (bf16[384,256]{1,0:T(8,128)(2,1)S(1)}, bf16[384,256]{1,0:T(8,128)(2,1)S(1)}, u32[]{:S(2)}, u32[]{:S(2)}) collective-permute-start(bf16[384,256]{1,0:T(8,128)(2,1)S(1)} %get-tuple-element.94), channel_id=1, source_target_pairs={{0,106},{1,63},{2,104},{3,61},{4,110},{5,59},{6,108},{7,57},{8,98}... | collective-permute-start | bytes 589832 | tf_op jit(solution)/shard_map/ppermute | solution.py:633
  53.0 9.8 %collective-permute-start.8 = (bf16[384,256]{1,0:T(8,128)(2,1)S(1)}, bf16[384,256]{1,0:T(8,128)(2,1)S(1)}, u32[]{:S(2)}, u32[]{:S(2)}) collective-permute-start(bf16[384,256]{1,0:T(8,128)(2,1)S(1)} %get-tuple-element.95), channel_id=1, source_target_pairs={{0,10},{1,31},{2,8},{3,29},{4,14},{5,27},{6,12},{7,25},{8,2},{9,23... | collective-permute-start | bytes 589832 | tf_op jit(solution)/shard_map/ppermute | solution.py:633
  56.1 10.4 %collective-permute-start.9 = (bf16[384,256]{1,0:T(8,128)(2,1)S(1)}, bf16[384,256]{1,0:T(8,128)(2,1)S(1)}, u32[]{:S(2)}, u32[]{:S(2)}) collective-permute-start(bf16[384,256]{1,0:T(8,128)(2,1)S(1)} %get-tuple-element.96), channel_id=1, source_target_pairs={{0,98},{1,39},{2,96},{3,37},{4,102},{5,35},{6,100},{7,33},{8,106},... | collective-permute-start | bytes 589832 | tf_op jit(solution)/shard_map/ppermute | solution.py:633
  57.1 9.3 %collective-permute-start.10 = (bf16[384,256]{1,0:T(8,128)(2,1)S(1)}, bf16[384,256]{1,0:T(8,128)(2,1)S(1)}, u32[]{:S(2)}, u32[]{:S(2)}) collective-permute-start(bf16[384,256]{1,0:T(8,128)(2,1)S(1)} %get-tuple-element.97), channel_id=1, source_target_pairs={{0,104},{1,57},{2,106},{3,59},{4,108},{5,61},{6,110},{7,63},{8,96}... | collective-permute-start | bytes 589832 | tf_op jit(solution)/shard_map/ppermute | solution.py:633
  66.6 3.5 %collective-permute-start.11 = (bf16[192,256]{1,0:T(8,128)(2,1)S(1)}, bf16[192,256]{1,0:T(8,128)(2,1)S(1)}, u32[]{:S(2)}, u32[]{:S(2)}) collective-permute-start(bf16[192,256]{1,0:T(8,128)(2,1)S(1)} %get-tuple-element.98.mine), channel_id=1, source_target_pairs={{0,6},{1,3},{2,4},{3,1},{4,2},{5,7},{6,0},{7,5},{8,14},{9,11},{10,... | collective-permute-start | bytes 294920 | tf_op jit(solution)/shard_map/ppermute | solution.py:633
  66.7 3.6 %collective-permute-start.14 = (bf16[192,256]{1,0:T(8,128)(2,1)S(1)}, bf16[192,256]{1,0:T(8,128)(2,1)S(1)}, u32[]{:S(2)}, u32[]{:S(2)}) collective-permute-start(bf16[192,256]{1,0:T(8,128)(2,1)S(1)} %get-tuple-element.99.mine), channel_id=1, source_target_pairs={{0,24},{1,9},{2,26},{3,11},{4,28},{5,13},{6,30},{7,15},{8,16},{9,1... | collective-permute-start | bytes 294920 | tf_op jit(solution)/shard_map/ppermute | solution.py:633
  70.2 3.5 %collective-permute-start.12 = (bf16[192,256]{1,0:T(8,128)(2,1)S(1)}, bf16[192,256]{1,0:T(8,128)(2,1)S(1)}, u32[]{:S(2)}, u32[]{:S(2)}) collective-permute-start(bf16[192,256]{1,0:T(8,128)(2,1)S(1)} %shard_map.344.mine), channel_id=1, source_target_pairs={{0,24},{1,9},{2,26},{3,11},{4,28},{5,13},{6,30},{7,15},{8,16},{9,1... | collective-permute-start | bytes 294920 | tf_op jit(solution)/shard_map/ppermute | solution.py:633
  70.4 5.4 %collective-permute-start.15 = (bf16[192,256]{1,0:T(8,128)(2,1)S(1)}, bf16[192,256]{1,0:T(8,128)(2,1)S(1)}, u32[]{:S(2)}, u32[]{:S(2)}) collective-permute-start(bf16[192,256]{1,0:T(8,128)(2,1)S(1)} %shard_map.346.mine), channel_id=1, source_target_pairs={{0,32},{1,97},{2,34},{3,99},{4,36},{5,101},{6,38},{7,103},{8,40},{... | collective-permute-start | bytes 294920 | tf_op jit(solution)/shard_map/ppermute | solution.py:633
  73.8 4.8 %collective-permute-start.13 = (bf16[192,256]{1,0:T(8,128)(2,1)S(1)}, bf16[192,256]{1,0:T(8,128)(2,1)S(1)}, u32[]{:S(2)}, u32[]{:S(2)}) collective-permute-start(bf16[192,256]{1,0:T(8,128)(2,1)S(1)} %shard_map.345.mine_a), channel_id=1, source_target_pairs={{0,32},{1,97},{2,34},{3,99},{4,36},{5,101},{6,38},{7,103},{8,40},{... | collective-permute-start | bytes 294920 | tf_op jit(solution)/shard_map/ppermute | solution.py:633
  75.8 3.5 %collective-permute-start.16 = (bf16[192,256]{1,0:T(8,128)(2,1)S(1)}, bf16[192,256]{1,0:T(8,128)(2,1)S(1)}, u32[]{:S(2)}, u32[]{:S(2)}) collective-permute-start(bf16[192,256]{1,0:T(8,128)(2,1)S(1)} %shard_map.347.mine_b), channel_id=1, source_target_pairs={{0,6},{1,3},{2,4},{3,1},{4,2},{5,7},{6,0},{7,5},{8,14},{9,11},{10,... | collective-permute-start | bytes 294920 | tf_op jit(solution)/shard_map/ppermute | solution.py:633
  79.4 21.8 %copy-start = (f32[256,1024]{1,0:T(8,128)S(1)}, f32[256,1024]{1,0:T(8,128)}, u32[]{:S(2)}) copy-start(f32[256,1024]{1,0:T(8,128)} %emb.5) | copy-start | bytes 3145732
  79.4 21.8 %copy-start.1 = (bf16[1024,256]{1,0:T(8,128)(2,1)S(1)}, bf16[1024,256]{1,0:T(8,128)(2,1)}, u32[]{:S(2)}) copy-start(bf16[1024,256]{1,0:T(8,128)(2,1)} %dense.5) | copy-start | bytes 1572868
  79.4 8.2 %collective-permute-start.23 = (bf16[384,256]{1,0:T(8,128)(2,1)S(1)}, bf16[384,256]{1,0:T(8,128)(2,1)S(1)}, u32[]{:S(2)}, u32[]{:S(2)}) collective-permute-start(bf16[384,256]{1,0:T(8,128)(2,1)S(1)} %shard_map.348.refs_0_), channel_id=1, source_target_pairs={{0,104},{1,57},{2,106},{3,59},{4,108},{5,61},{6,110},{7,63},{8,96}... | collective-permute-start | bytes 589832 | tf_op jit(solution)/shard_map/ppermute | solution.py:633
  80.1 9.4 %collective-permute-start.22 = (bf16[384,256]{1,0:T(8,128)(2,1)S(1)}, bf16[384,256]{1,0:T(8,128)(2,1)S(1)}, u32[]{:S(2)}, u32[]{:S(2)}) collective-permute-start(bf16[384,256]{1,0:T(8,128)(2,1)S(1)} %shard_map.348.refs_0_), channel_id=1, source_target_pairs={{0,98},{1,39},{2,96},{3,37},{4,102},{5,35},{6,100},{7,33},{8,106},... | collective-permute-start | bytes 589832 | tf_op jit(solution)/shard_map/ppermute | solution.py:633
  81.7 10.1 %collective-permute-start.21 = (bf16[384,256]{1,0:T(8,128)(2,1)S(1)}, bf16[384,256]{1,0:T(8,128)(2,1)S(1)}, u32[]{:S(2)}, u32[]{:S(2)}) collective-permute-start(bf16[384,256]{1,0:T(8,128)(2,1)S(1)} %shard_map.348.refs_0_), channel_id=1, source_target_pairs={{0,10},{1,31},{2,8},{3,29},{4,14},{5,27},{6,12},{7,25},{8,2},{9,23... | collective-permute-start | bytes 589832 | tf_op jit(solution)/shard_map/ppermute | solution.py:633
  85.5 8.9 %collective-permute-start.20 = (bf16[384,256]{1,0:T(8,128)(2,1)S(1)}, bf16[384,256]{1,0:T(8,128)(2,1)S(1)}, u32[]{:S(2)}, u32[]{:S(2)}) collective-permute-start(bf16[384,256]{1,0:T(8,128)(2,1)S(1)} %shard_map.348.refs_0_), channel_id=1, source_target_pairs={{0,106},{1,63},{2,104},{3,61},{4,110},{5,59},{6,108},{7,57},{8,98}... | collective-permute-start | bytes 589832 | tf_op jit(solution)/shard_map/ppermute | solution.py:633
  86.7 7.7 %collective-permute-start.19 = (bf16[384,256]{1,0:T(8,128)(2,1)S(1)}, bf16[384,256]{1,0:T(8,128)(2,1)S(1)}, u32[]{:S(2)}, u32[]{:S(2)}) collective-permute-start(bf16[384,256]{1,0:T(8,128)(2,1)S(1)} %shard_map.348.refs_0_), channel_id=1, source_target_pairs={{0,96},{1,33},{2,98},{3,35},{4,100},{5,37},{6,102},{7,39},{8,104},... | collective-permute-start | bytes 589832 | tf_op jit(solution)/shard_map/ppermute | solution.py:633
  87.7 6.8 %collective-permute-start.18 = (bf16[384,256]{1,0:T(8,128)(2,1)S(1)}, bf16[384,256]{1,0:T(8,128)(2,1)S(1)}, u32[]{:S(2)}, u32[]{:S(2)}) collective-permute-start(bf16[384,256]{1,0:T(8,128)(2,1)S(1)} %shard_map.348.refs_0_), channel_id=1, source_target_pairs={{0,8},{1,25},{2,10},{3,27},{4,12},{5,29},{6,14},{7,31},{8,0},{9,17... | collective-permute-start | bytes 589832 | tf_op jit(solution)/shard_map/ppermute | solution.py:633
  89.5 7.3 %collective-permute-start.17 = (bf16[384,256]{1,0:T(8,128)(2,1)S(1)}, bf16[384,256]{1,0:T(8,128)(2,1)S(1)}, u32[]{:S(2)}, u32[]{:S(2)}) collective-permute-start(bf16[384,256]{1,0:T(8,128)(2,1)S(1)} %shard_map.348.refs_0_), channel_id=1, source_target_pairs={{0,2},{1,7},{2,0},{3,5},{4,6},{5,3},{6,4},{7,1},{8,10},{9,15},{10,... | collective-permute-start | bytes 589832 | tf_op jit(solution)/shard_map/ppermute | solution.py:633
  96.8 7.4 %collective-permute-start.24 = (bf16[3072,256]{1,0:T(8,128)(2,1)S(1)}, bf16[3072,256]{1,0:T(8,128)(2,1)S(1)}, u32[]{:S(2)}, u32[]{:S(2)}) collective-permute-start(bf16[3072,256]{1,0:T(8,128)(2,1)S(1)} %shard_map.349.mine), channel_id=1, source_target_pairs={{0,1},{1,0},{2,3},{3,2},{4,5},{5,4},{6,7},{7,6},{8,9},{9,8},{10,11... | collective-permute-start | bytes 4718600 | tf_op jit(solution)/shard_map/ppermute | solution.py:516
where the time goes:
time: 107 us
  starting transfers between devices  39.7 us (37%)
  Pallas kernels  38.6 us (36%)
  waiting for transfers between devices  23.2 us (22%)
  local copies, waits for them, and re-layouts  4.36 us (4%)
    ppermute x20, starting transfers between devices, exchange(): return lax.ppermute(block, 'batch', pairs)  32.7 us
    pallas_call x1, Pallas kernels, run(): pl.pallas_call(kernel_body, in_specs=[SMEM, SMEM] + [ANY] * 7 + [VMEM] *...  31.6 us
    ppermute x20, waiting for transfers between devices, exchange(): return lax.ppermute(block, 'batch', pairs)  18.6 us
    ppermute x5, starting transfers between devices, swap(): return lax.ppermute(block, 'batch', [(i, i ^ 1) for i in range(count)])  6.95 us
    ppermute x5, waiting for transfers between devices, swap(): return lax.ppermute(block, 'batch', [(i, i ^ 1) for i in range(count)])  4.58 us
    unnamed x12, local copies, waits for them, and re-layouts  3.07 us
    pallas_call x1, Pallas kernels, finish(): pl.pallas_call(finish_other_body, in_specs=[SMEM, VMEM, VMEM, ANY, ANY] +...  2.46 us
    pallas_call x1, Pallas kernels, finish(): pl.pallas_call(finish_own_body, in_specs=[SMEM, VMEM, ANY, ANY], out_spec...  2.45 us
  transfers between devices with their start and end apart: 25, of which 12 were waited for; matrix products, arithmetic and copies ran while one was open for 0% of the time, Pallas kernels for 4%

commit v1 on v0

--- a/solution.py
+++ b/solution.py
@@ -530,7 +530,7 @@
 def join(place, mine_r, mine_i, got_r, got_i):
     return pl.pallas_call(
         join_body,
-        in_specs=[SMEM, ANY, ANY, ANY, VMEM],
+        in_specs=[SMEM, ANY, ANY, VMEM, VMEM],
         out_specs=[ANY, ANY],
         out_shape=[shape(*mine_r.shape, kind=BF), shape(*mine_i.shape)],
         input_output_aliases={1: 0, 2: 1},
@@ -644,8 +644,9 @@
 def all_sum(keep, other, device, meanwhile, afterwards):
     bits = [(place + 1) // 2 % 2 for place in lines(device)]
     piece = (bits[0] + 2 * bits[1] + 4 * bits[2]).reshape(1).astype(jnp.int32)
-    sends = small_call(add_body, EIGHTH, EIGHT, piece, nearby(keep), other)
-    arrived = meanwhile(sends[0])
+    keep, other = lax.optimization_barrier((nearby(keep), other))
+    arrived = meanwhile(other)
+    sends = small_call(add_body, EIGHTH, EIGHT, piece, keep, other)
     early, late = EVENLY[:3], EVENLY[3:]
     got = [exchange(sends[mask], near(mask)) for mask in early]
     held, arrived = lax.optimization_barrier(([sends[mask] for mask in late], arrived))

time: 107 us -> 107 us (level)
  waiting for transfers between devices: 23.2 us -> 22 us
  Pallas kernels: 38.6 us -> 39.8 us
    pallas_call x1, Pallas kernels: 1.16 us -> 2.36 us  [join(): pl.pallas_call(join_body, in_specs=[SMEM, ANY, ANY, VMEM, VMEM], out_spec...]
    ppermute x20, waiting for transfers between devices: 18.6 us -> 17.5 us  [exchange(): return lax.ppermute(block, 'batch', pairs)]
    unnamed x12 -> x8, local copies, waits for them, and re-layouts: 3.07 us -> 2.39 us
  transfers between devices with their start and end apart: 25 -> 25, of which waited for: 12 -> 11; matrix products, arithmetic and copies ran while one was open for 0% -> 0% of each run, Pallas kernels for 4% -> 5%
where the time goes in v1:
time: 107 us; the launch traced here: 106 us
  Pallas kernels  39.8 us (37%)
  starting transfers between devices  39.7 us (37%)
  waiting for transfers between devices  22 us (21%)
  local copies, waits for them, and re-layouts  3.68 us (3%)
    ppermute x20, starting transfers between devices, exchange(): return lax.ppermute(block, 'batch', pairs)  32.7 us
    pallas_call x1, Pallas kernels, run(): pl.pallas_call(kernel_body, in_specs=[SMEM, SMEM] + [ANY] * 7 + [VMEM] *...  31.6 us
    ppermute x20, waiting for transfers between devices, exchange(): return lax.ppermute(block, 'batch', pairs)  17.5 us
    ppermute x5, starting transfers between devices, swap(): return lax.ppermute(block, 'batch', [(i, i ^ 1) for i in range(count)])  7.03 us
    ppermute x5, waiting for transfers between devices, swap(): return lax.ppermute(block, 'batch', [(i, i ^ 1) for i in range(count)])  4.58 us
    pallas_call x1, Pallas kernels, finish(): pl.pallas_call(finish_other_body, in_specs=[SMEM, VMEM, VMEM, ANY, ANY] +...  2.46 us
    pallas_call x1, Pallas kernels, finish(): pl.pallas_call(finish_own_body, in_specs=[SMEM, VMEM, ANY, ANY], out_spec...  2.45 us
    unnamed x8, local copies, waits for them, and re-layouts  2.39 us
  transfers between devices with their start and end apart: 25, of which 11 were waited for; matrix products, arithmetic and copies ran while one was open for 0% of the time, Pallas kernels for 5%

profile of v1, /device:TPU:1, one launch (start us, length us, event | category | flops | bytes accessed | tf_op | source)
XLA Modules:
  0.0 106.3 jit_solution(13822004332546674893)
XLA Ops:
  0.7 1.3 %constant_dynamic-slice_fusion = (bf16[8,128,256]{2,1,0:T(8,128)(2,1)S(1)}, bf16[8,128,256]{2,1,0:T(8,128)(2,1)S(1)}) fusion(bf16[16,128,256]{2,1,0:T(8,128)(2,1)} %bitcast.16, s32[]{:T(128)S(6)} %select_n.72, bf16[16,128,256]{2,1,0:T(8,128)(2,1)} %bitcast.14), kind=kLoop, calls=%fused_computation.1 | loop fusion | bytes 2097156 | tf_op jit(solution)/shard_map/dynamic_slice | solution.py:780
  2.1 1.5 %collective-permute-start = (bf16[16,128,256]{2,1,0:T(8,128)(2,1)S(1)}, bf16[16,128,256]{2,1,0:T(8,128)(2,1)S(1)}, u32[]{:S(2)}, u32[]{:S(2)}) collective-permute-start(bf16[16,128,256]{2,1,0:T(8,128)(2,1)S(1)} %pad_maximum_fusion), channel_id=1, source_target_pairs={{0,1},{1,0},{2,3},{3,2},{4,5},{5,4},{6,7},{7,6},{8,9},{9,8},{10,11... | collective-permute-start | bytes 3145736 | tf_op jit(solution)/shard_map/ppermute | solution.py:516
  3.6 2.3 %collective-permute-done.got = bf16[16,128,256]{2,1,0:T(8,128)(2,1)S(1)} collective-permute-done((bf16[16,128,256]{2,1,0:T(8,128)(2,1)S(1)}, bf16[16,128,256]{2,1,0:T(8,128)(2,1)S(1)}, u32[]{:S(2)}, u32[]{:S(2)}) %collective-permute-start) | collective-permute-done | bytes 1048608 | tf_op jit(solution)/shard_map/ppermute | solution.py:516
  6.8 31.6 %shard_map.339 = (bf16[16,128,256]{2,1,0:T(8,128)(2,1)}, bf16[8,128,256]{2,1,0:T(8,128)(2,1)}, f32[16,128,256]{2,1,0:T(8,128)}, bf16[8,128,256]{2,1,0:T(8,128)(2...) custom-call(s32[1]{0:T(128)} %bitcast.1.place, s32[1024]{0:T(1024)} %steps.1, bf16[16,128,256]{2,1,0:T(8,128)(2,1)} %bitcast.15, ...), custom_call_target="tpu_custom_call" | custom-call | flops 20000000000 | bytes 20000000 | tf_op jit(solution)/shard_map/pallas_call | solution.py:458
  39.0 1.4 %copy-done.2 = bf16[3072,256]{1,0:T(8,128)(2,1)S(1)} copy-done((bf16[3072,256]{1,0:T(8,128)(2,1)S(1)}, bf16[3072,256]{1,0:T(8,128)(2,1)}, u32[]{:S(2)}) %copy-start.2) | copy-done | bytes 1572888
  40.5 1.7 %collective-permute-done.1.other = bf16[3072,256]{1,0:T(8,128)(2,1)S(1)} collective-permute-done((bf16[3072,256]{1,0:T(8,128)(2,1)}, bf16[3072,256]{1,0:T(8,128)(2,1)S(1)}, u32[]{:S(2)}, u32[]{:S(2)}) %collective-permute-start.1) | collective-permute-done | bytes 1572896 | tf_op jit(solution)/shard_map/ppermute | solution.py:516
  43.1 3.9 %collective-permute-start.4 = (bf16[384,256]{1,0:T(8,128)(2,1)S(1)}, bf16[384,256]{1,0:T(8,128)(2,1)S(1)}, u32[]{:S(2)}, u32[]{:S(2)}) collective-permute-start(bf16[384,256]{1,0:T(8,128)(2,1)S(1)} %get-tuple-element.95), channel_id=1, source_target_pairs={{0,2},{1,7},{2,0},{3,5},{4,6},{5,3},{6,4},{7,1},{8,10},{9,15},{10,... | collective-permute-start | bytes 589832 | tf_op jit(solution)/shard_map/ppermute | solution.py:633
  47.0 2.5 %collective-permute-start.5 = (bf16[384,256]{1,0:T(8,128)(2,1)S(1)}, bf16[384,256]{1,0:T(8,128)(2,1)S(1)}, u32[]{:S(2)}, u32[]{:S(2)}) collective-permute-start(bf16[384,256]{1,0:T(8,128)(2,1)S(1)} %get-tuple-element.96), channel_id=1, source_target_pairs={{0,8},{1,25},{2,10},{3,27},{4,12},{5,29},{6,14},{7,31},{8,0},{9,17... | collective-permute-start | bytes 589832 | tf_op jit(solution)/shard_map/ppermute | solution.py:633
  49.5 1.3 %collective-permute-start.6 = (bf16[384,256]{1,0:T(8,128)(2,1)S(1)}, bf16[384,256]{1,0:T(8,128)(2,1)S(1)}, u32[]{:S(2)}, u32[]{:S(2)}) collective-permute-start(bf16[384,256]{1,0:T(8,128)(2,1)S(1)} %get-tuple-element.97), channel_id=1, source_target_pairs={{0,96},{1,33},{2,98},{3,35},{4,100},{5,37},{6,102},{7,39},{8,104},... | collective-permute-start | bytes 589832 | tf_op jit(solution)/shard_map/ppermute | solution.py:633
  50.8 1.5 %collective-permute-start.7 = (bf16[384,256]{1,0:T(8,128)(2,1)S(1)}, bf16[384,256]{1,0:T(8,128)(2,1)S(1)}, u32[]{:S(2)}, u32[]{:S(2)}) collective-permute-start(bf16[384,256]{1,0:T(8,128)(2,1)S(1)} %get-tuple-element.98), channel_id=1, source_target_pairs={{0,106},{1,63},{2,104},{3,61},{4,110},{5,59},{6,108},{7,57},{8,98}... | collective-permute-start | bytes 589832 | tf_op jit(solution)/shard_map/ppermute | solution.py:633
  52.3 3.2 %collective-permute-start.8 = (bf16[384,256]{1,0:T(8,128)(2,1)S(1)}, bf16[384,256]{1,0:T(8,128)(2,1)S(1)}, u32[]{:S(2)}, u32[]{:S(2)}) collective-permute-start(bf16[384,256]{1,0:T(8,128)(2,1)S(1)} %get-tuple-element.99), channel_id=1, source_target_pairs={{0,10},{1,31},{2,8},{3,29},{4,14},{5,27},{6,12},{7,25},{8,2},{9,23... | collective-permute-start | bytes 589832 | tf_op jit(solution)/shard_map/ppermute | solution.py:633
  55.5 1.1 %collective-permute-start.9 = (bf16[384,256]{1,0:T(8,128)(2,1)S(1)}, bf16[384,256]{1,0:T(8,128)(2,1)S(1)}, u32[]{:S(2)}, u32[]{:S(2)}) collective-permute-start(bf16[384,256]{1,0:T(8,128)(2,1)S(1)} %get-tuple-element.100), channel_id=1, source_target_pairs={{0,98},{1,39},{2,96},{3,37},{4,102},{5,35},{6,100},{7,33},{8,106},... | collective-permute-start | bytes 589832 | tf_op jit(solution)/shard_map/ppermute | solution.py:633
  56.6 1.7 %collective-permute-start.10 = (bf16[384,256]{1,0:T(8,128)(2,1)S(1)}, bf16[384,256]{1,0:T(8,128)(2,1)S(1)}, u32[]{:S(2)}, u32[]{:S(2)}) collective-permute-start(bf16[384,256]{1,0:T(8,128)(2,1)S(1)} %get-tuple-element.101), channel_id=1, source_target_pairs={{0,104},{1,57},{2,106},{3,59},{4,108},{5,61},{6,110},{7,63},{8,96}... | collective-permute-start | bytes 589832 | tf_op jit(solution)/shard_map/ppermute | solution.py:633
  58.2 2.4 %shard_map.342 = (bf16[16,128,256]{2,1,0:T(8,128)(2,1)}, f32[16,128,256]{2,1,0:T(8,128)}) custom-call(s32[1]{0:T(128)} %bitcast.1.place, bf16[16,128,256]{2,1,0:T(8,128)(2,1)} %get-tuple-element.78.mine_r, f32[16,128,256]{2,1,0:T(8,128)} %get-tuple-element.79.mine_i, ...), custom_call_target="tpu_custom_call", output_to_operand_aliasing={{0}: (1, {}), {1}: (2, {})} | custom-call | bytes 4000000 | tf_op jit(solution)/shard_map/pallas_call | solution.py:531
  60.6 1.5 %collective-permute-done.8.refs_5_ = bf16[384,256]{1,0:T(8,128)(2,1)S(1)} collective-permute-done((bf16[384,256]{1,0:T(8,128)(2,1)S(1)}, bf16[384,256]{1,0:T(8,128)(2,1)S(1)}, u32[]{:S(2)}, u32[]{:S(2)}) %collective-permute-start.8) | collective-permute-done | bytes 196640 | tf_op jit(solution)/shard_map/ppermute | solution.py:633
  62.2 3.6 %collective-permute-done.9.refs_6_ = bf16[384,256]{1,0:T(8,128)(2,1)S(1)} collective-permute-done((bf16[384,256]{1,0:T(8,128)(2,1)S(1)}, bf16[384,256]{1,0:T(8,128)(2,1)S(1)}, u32[]{:S(2)}, u32[]{:S(2)}) %collective-permute-start.9) | collective-permute-done | bytes 196640 | tf_op jit(solution)/shard_map/ppermute | solution.py:633
  66.2 3.4 %collective-permute-done.11.got = bf16[192,256]{1,0:T(8,128)(2,1)S(1)} collective-permute-done((bf16[192,256]{1,0:T(8,128)(2,1)S(1)}, bf16[192,256]{1,0:T(8,128)(2,1)S(1)}, u32[]{:S(2)}, u32[]{:S(2)}) %collective-permute-start.11) | collective-permute-done | bytes 98336 | tf_op jit(solution)/shard_map/ppermute | solution.py:633
  69.7 1.9 %collective-permute-start.15 = (bf16[192,256]{1,0:T(8,128)(2,1)S(1)}, bf16[192,256]{1,0:T(8,128)(2,1)S(1)}, u32[]{:S(2)}, u32[]{:S(2)}) collective-permute-start(bf16[192,256]{1,0:T(8,128)(2,1)S(1)} %shard_map.346.mine), channel_id=1, source_target_pairs={{0,32},{1,97},{2,34},{3,99},{4,36},{5,101},{6,38},{7,103},{8,40},{... | collective-permute-start | bytes 294920 | tf_op jit(solution)/shard_map/ppermute | solution.py:633
  71.7 1.5 %collective-permute-done.12.got = bf16[192,256]{1,0:T(8,128)(2,1)S(1)} collective-permute-done((bf16[192,256]{1,0:T(8,128)(2,1)S(1)}, bf16[192,256]{1,0:T(8,128)(2,1)S(1)}, u32[]{:S(2)}, u32[]{:S(2)}) %collective-permute-start.12) | collective-permute-done | bytes 98336 | tf_op jit(solution)/shard_map/ppermute | solution.py:633
  73.2 1.9 %collective-permute-start.13 = (bf16[192,256]{1,0:T(8,128)(2,1)S(1)}, bf16[192,256]{1,0:T(8,128)(2,1)S(1)}, u32[]{:S(2)}, u32[]{:S(2)}) collective-permute-start(bf16[192,256]{1,0:T(8,128)(2,1)S(1)} %shard_map.345.mine_a), channel_id=1, source_target_pairs={{0,32},{1,97},{2,34},{3,99},{4,36},{5,101},{6,38},{7,103},{8,40},{... | collective-permute-start | bytes 294920 | tf_op jit(solution)/shard_map/ppermute | solution.py:633
  75.1 1.1 %collective-permute-start.16 = (bf16[192,256]{1,0:T(8,128)(2,1)S(1)}, bf16[192,256]{1,0:T(8,128)(2,1)S(1)}, u32[]{:S(2)}, u32[]{:S(2)}) collective-permute-start(bf16[192,256]{1,0:T(8,128)(2,1)S(1)} %shard_map.347.mine_b), channel_id=1, source_target_pairs={{0,6},{1,3},{2,4},{3,1},{4,2},{5,7},{6,0},{7,5},{8,14},{9,11},{10,... | collective-permute-start | bytes 294920 | tf_op jit(solution)/shard_map/ppermute | solution.py:633
  76.2 1.7 %collective-permute-done.13.got_a = bf16[192,256]{1,0:T(8,128)(2,1)S(1)} collective-permute-done((bf16[192,256]{1,0:T(8,128)(2,1)S(1)}, bf16[192,256]{1,0:T(8,128)(2,1)S(1)}, u32[]{:S(2)}, u32[]{:S(2)}) %collective-permute-start.13) | collective-permute-done | bytes 98336 | tf_op jit(solution)/shard_map/ppermute | solution.py:633
  79.5 1.5 %collective-permute-start.22 = (bf16[384,256]{1,0:T(8,128)(2,1)S(1)}, bf16[384,256]{1,0:T(8,128)(2,1)S(1)}, u32[]{:S(2)}, u32[]{:S(2)}) collective-permute-start(bf16[384,256]{1,0:T(8,128)(2,1)S(1)} %shard_map.348.refs_0_), channel_id=1, source_target_pairs={{0,98},{1,39},{2,96},{3,37},{4,102},{5,35},{6,100},{7,33},{8,106},... | collective-permute-start | bytes 589832 | tf_op jit(solution)/shard_map/ppermute | solution.py:633
  81.0 3.8 %collective-permute-start.21 = (bf16[384,256]{1,0:T(8,128)(2,1)S(1)}, bf16[384,256]{1,0:T(8,128)(2,1)S(1)}, u32[]{:S(2)}, u32[]{:S(2)}) collective-permute-start(bf16[384,256]{1,0:T(8,128)(2,1)S(1)} %shard_map.348.refs_0_), channel_id=1, source_target_pairs={{0,10},{1,31},{2,8},{3,29},{4,14},{5,27},{6,12},{7,25},{8,2},{9,23... | collective-permute-start | bytes 589832 | tf_op jit(solution)/shard_map/ppermute | solution.py:633
  84.8 1.3 %collective-permute-start.20 = (bf16[384,256]{1,0:T(8,128)(2,1)S(1)}, bf16[384,256]{1,0:T(8,128)(2,1)S(1)}, u32[]{:S(2)}, u32[]{:S(2)}) collective-permute-start(bf16[384,256]{1,0:T(8,128)(2,1)S(1)} %shard_map.348.refs_0_), channel_id=1, source_target_pairs={{0,106},{1,63},{2,104},{3,61},{4,110},{5,59},{6,108},{7,57},{8,98}... | collective-permute-start | bytes 589832 | tf_op jit(solution)/shard_map/ppermute | solution.py:633
  87.0 1.9 %collective-permute-start.18 = (bf16[384,256]{1,0:T(8,128)(2,1)S(1)}, bf16[384,256]{1,0:T(8,128)(2,1)S(1)}, u32[]{:S(2)}, u32[]{:S(2)}) collective-permute-start(bf16[384,256]{1,0:T(8,128)(2,1)S(1)} %shard_map.348.refs_0_), channel_id=1, source_target_pairs={{0,8},{1,25},{2,10},{3,27},{4,12},{5,29},{6,14},{7,31},{8,0},{9,17... | collective-permute-start | bytes 589832 | tf_op jit(solution)/shard_map/ppermute | solution.py:633
  88.9 2.2 %collective-permute-start.17 = (bf16[384,256]{1,0:T(8,128)(2,1)S(1)}, bf16[384,256]{1,0:T(8,128)(2,1)S(1)}, u32[]{:S(2)}, u32[]{:S(2)}) collective-permute-start(bf16[384,256]{1,0:T(8,128)(2,1)S(1)} %shard_map.348.refs_0_), channel_id=1, source_target_pairs={{0,2},{1,7},{2,0},{3,5},{4,6},{5,3},{6,4},{7,1},{8,10},{9,15},{10,... | collective-permute-start | bytes 589832 | tf_op jit(solution)/shard_map/ppermute | solution.py:633
  91.1 2.7 %collective-permute-done.20.refs_4_ = bf16[384,256]{1,0:T(8,128)(2,1)S(1)} collective-permute-done((bf16[384,256]{1,0:T(8,128)(2,1)S(1)}, bf16[384,256]{1,0:T(8,128)(2,1)S(1)}, u32[]{:S(2)}, u32[]{:S(2)}) %collective-permute-start.20) | collective-permute-done | bytes 196640 | tf_op jit(solution)/shard_map/ppermute | solution.py:633
  93.8 2.3 %collective-permute-done.17.refs_1_ = bf16[384,256]{1,0:T(8,128)(2,1)S(1)} collective-permute-done((bf16[384,256]{1,0:T(8,128)(2,1)S(1)}, bf16[384,256]{1,0:T(8,128)(2,1)S(1)}, u32[]{:S(2)}, u32[]{:S(2)}) %collective-permute-start.17) | collective-permute-done | bytes 196640 | tf_op jit(solution)/shard_map/ppermute | solution.py:633
  96.1 4.5 %collective-permute-start.24 = (bf16[3072,256]{1,0:T(8,128)(2,1)S(1)}, bf16[3072,256]{1,0:T(8,128)(2,1)S(1)}, u32[]{:S(2)}, u32[]{:S(2)}) collective-permute-start(bf16[3072,256]{1,0:T(8,128)(2,1)S(1)} %shard_map.349.mine), channel_id=1, source_target_pairs={{0,1},{1,0},{2,3},{3,2},{4,5},{5,4},{6,7},{7,6},{8,9},{9,8},{10,11... | collective-permute-start | bytes 4718600 | tf_op jit(solution)/shard_map/ppermute | solution.py:516
  100.7 2.5 %shard_map.350 = (f32[9,256,256]{2,1,0:T(8,128)}, f32[256,768]{1,0:T(8,128)}, f32[256,256]{1,0:T(8,128)}, f32[9,256,256]{2,1,0:T(8,128)}, f32[1024,256]{1,0:T(8,128)}, /*index=5*/f32[256,1024]{1,0:T(8,128)}) custom-call(s32[1]{0:T(128)} %bitcast.1.place, bf16[3072,256]{1,0:T(8,128)(2,1)S(1)} %shard_map.349.mine, f32[256,1024]{1,0:T(8,128)S(1)} %copy-done, ...), custom_call_target="tpu_custom_call" | custom-call | flops 100000000 | bytes 6000000 | tf_op jit(solution)/shard_map/pallas_call | solution.py:749
  103.7 2.5 %shard_map.351 = (f32[9,256,256]{2,1,0:T(8,128)}, f32[256,768]{1,0:T(8,128)}, f32[256,256]{1,0:T(8,128)}, f32[9,256,256]{2,1,0:T(8,128)}, f32[1024,256]{1,0:T(8,...) custom-call(s32[1]{0:T(128)} %bitcast.1.place, ...), custom_call_target="tpu_custom_call", output_to_operand_aliasing={{0}: (5, {}), {1}: (6, {}), {2}: (7, {}), {3}: (8, {}), {4}... | custom-call | flops 100000000 | bytes 6000000 | tf_op jit(solution)/shard_map/pallas_call | solution.py:756
  (41 shorter events, 6.3 us)
Async XLA Ops:
  2.1 3.8 %collective-permute-start = (bf16[16,128,256]{2,1,0:T(8,128)(2,1)S(1)}, bf16[16,128,256]{2,1,0:T(8,128)(2,1)S(1)}, u32[]{:S(2)}, u32[]{:S(2)}) collective-permute-start(bf16[16,128,256]{2,1,0:T(8,128)(2,1)S(1)} %pad_maximum_fusion), channel_id=1, source_target_pairs={{0,1},{1,0},{2,3},{3,2},{4,5},{5,4},{6,7},{7,6},{8,9},{9,8},{10,11... | collective-permute-start | bytes 3145736 | tf_op jit(solution)/shard_map/ppermute | solution.py:516
  5.9 1.0 copy-start.3
  38.4 3.7 %collective-permute-start.1 = (bf16[3072,256]{1,0:T(8,128)(2,1)}, bf16[3072,256]{1,0:T(8,128)(2,1)S(1)}, u32[]{:S(2)}, u32[]{:S(2)}) collective-permute-start(bf16[3072,256]{1,0:T(8,128)(2,1)} %get-tuple-element.74), channel_id=1, source_target_pairs={{0,1},{1,0},{2,3},{3,2},{4,5},{5,4},{6,7},{7,6},{8,9},{9,8},{10,11... | collective-permute-start | bytes 4718600 | tf_op jit(solution)/shard_map/ppermute | solution.py:516
  38.9 1.4 %copy-start.2 = (bf16[3072,256]{1,0:T(8,128)(2,1)S(1)}, bf16[3072,256]{1,0:T(8,128)(2,1)}, u32[]{:S(2)}) copy-start(bf16[3072,256]{1,0:T(8,128)(2,1)} %get-tuple-element.73.x) | copy-start | bytes 4718596
  42.2 8.6 %collective-permute-start.2 = (bf16[8,128,256]{2,1,0:T(8,128)(2,1)}, bf16[8,128,256]{2,1,0:T(8,128)(2,1)}, u32[]{:S(2)}, u32[]{:S(2)}) collective-permute-start(bf16[8,128,256]{2,1,0:T(8,128)(2,1)} %get-tuple-element.86), channel_id=1, source_target_pairs={{0,1},{1,0},{2,3},{3,2},{4,5},{5,4},{6,7},{7,6},{8,9},{9,8},{10,11... | collective-permute-start | bytes 1572872 | tf_op jit(solution)/shard_map/ppermute | solution.py:516
  42.6 8.2 %collective-permute-start.3 = (bf16[8,128,256]{2,1,0:T(8,128)(2,1)}, bf16[8,128,256]{2,1,0:T(8,128)(2,1)}, u32[]{:S(2)}, u32[]{:S(2)}) collective-permute-start(bf16[8,128,256]{2,1,0:T(8,128)(2,1)} %get-tuple-element.87), channel_id=1, source_target_pairs={{0,1},{1,0},{2,3},{3,2},{4,5},{5,4},{6,7},{7,6},{8,9},{9,8},{10,11... | collective-permute-start | bytes 1572872 | tf_op jit(solution)/shard_map/ppermute | solution.py:516
  43.1 12.4 %collective-permute-start.4 = (bf16[384,256]{1,0:T(8,128)(2,1)S(1)}, bf16[384,256]{1,0:T(8,128)(2,1)S(1)}, u32[]{:S(2)}, u32[]{:S(2)}) collective-permute-start(bf16[384,256]{1,0:T(8,128)(2,1)S(1)} %get-tuple-element.95), channel_id=1, source_target_pairs={{0,2},{1,7},{2,0},{3,5},{4,6},{5,3},{6,4},{7,1},{8,10},{9,15},{10,... | collective-permute-start | bytes 589832 | tf_op jit(solution)/shard_map/ppermute | solution.py:633
  47.0 9.6 %collective-permute-start.5 = (bf16[384,256]{1,0:T(8,128)(2,1)S(1)}, bf16[384,256]{1,0:T(8,128)(2,1)S(1)}, u32[]{:S(2)}, u32[]{:S(2)}) collective-permute-start(bf16[384,256]{1,0:T(8,128)(2,1)S(1)} %get-tuple-element.96), channel_id=1, source_target_pairs={{0,8},{1,25},{2,10},{3,27},{4,12},{5,29},{6,14},{7,31},{8,0},{9,17... | collective-permute-start | bytes 589832 | tf_op jit(solution)/shard_map/ppermute | solution.py:633
  49.5 11.1 %collective-permute-start.6 = (bf16[384,256]{1,0:T(8,128)(2,1)S(1)}, bf16[384,256]{1,0:T(8,128)(2,1)S(1)}, u32[]{:S(2)}, u32[]{:S(2)}) collective-permute-start(bf16[384,256]{1,0:T(8,128)(2,1)S(1)} %get-tuple-element.97), channel_id=1, source_target_pairs={{0,96},{1,33},{2,98},{3,35},{4,100},{5,37},{6,102},{7,39},{8,104},... | collective-permute-start | bytes 589832 | tf_op jit(solution)/shard_map/ppermute | solution.py:633
  50.8 9.8 %collective-permute-start.7 = (bf16[384,256]{1,0:T(8,128)(2,1)S(1)}, bf16[384,256]{1,0:T(8,128)(2,1)S(1)}, u32[]{:S(2)}, u32[]{:S(2)}) collective-permute-start(bf16[384,256]{1,0:T(8,128)(2,1)S(1)} %get-tuple-element.98), channel_id=1, source_target_pairs={{0,106},{1,63},{2,104},{3,61},{4,110},{5,59},{6,108},{7,57},{8,98}... | collective-permute-start | bytes 589832 | tf_op jit(solution)/shard_map/ppermute | solution.py:633
  52.3 9.9 %collective-permute-start.8 = (bf16[384,256]{1,0:T(8,128)(2,1)S(1)}, bf16[384,256]{1,0:T(8,128)(2,1)S(1)}, u32[]{:S(2)}, u32[]{:S(2)}) collective-permute-start(bf16[384,256]{1,0:T(8,128)(2,1)S(1)} %get-tuple-element.99), channel_id=1, source_target_pairs={{0,10},{1,31},{2,8},{3,29},{4,14},{5,27},{6,12},{7,25},{8,2},{9,23... | collective-permute-start | bytes 589832 | tf_op jit(solution)/shard_map/ppermute | solution.py:633
  55.5 10.3 %collective-permute-start.9 = (bf16[384,256]{1,0:T(8,128)(2,1)S(1)}, bf16[384,256]{1,0:T(8,128)(2,1)S(1)}, u32[]{:S(2)}, u32[]{:S(2)}) collective-permute-start(bf16[384,256]{1,0:T(8,128)(2,1)S(1)} %get-tuple-element.100), channel_id=1, source_target_pairs={{0,98},{1,39},{2,96},{3,37},{4,102},{5,35},{6,100},{7,33},{8,106},... | collective-permute-start | bytes 589832 | tf_op jit(solution)/shard_map/ppermute | solution.py:633
  56.6 9.2 %collective-permute-start.10 = (bf16[384,256]{1,0:T(8,128)(2,1)S(1)}, bf16[384,256]{1,0:T(8,128)(2,1)S(1)}, u32[]{:S(2)}, u32[]{:S(2)}) collective-permute-start(bf16[384,256]{1,0:T(8,128)(2,1)S(1)} %get-tuple-element.101), channel_id=1, source_target_pairs={{0,104},{1,57},{2,106},{3,59},{4,108},{5,61},{6,110},{7,63},{8,96}... | collective-permute-start | bytes 589832 | tf_op jit(solution)/shard_map/ppermute | solution.py:633
  66.0 3.5 %collective-permute-start.11 = (bf16[192,256]{1,0:T(8,128)(2,1)S(1)}, bf16[192,256]{1,0:T(8,128)(2,1)S(1)}, u32[]{:S(2)}, u32[]{:S(2)}) collective-permute-start(bf16[192,256]{1,0:T(8,128)(2,1)S(1)} %get-tuple-element.102.mine), channel_id=1, source_target_pairs={{0,6},{1,3},{2,4},{3,1},{4,2},{5,7},{6,0},{7,5},{8,14},{9,11},{10,... | collective-permute-start | bytes 294920 | tf_op jit(solution)/shard_map/ppermute | solution.py:633
  66.1 3.6 %collective-permute-start.14 = (bf16[192,256]{1,0:T(8,128)(2,1)S(1)}, bf16[192,256]{1,0:T(8,128)(2,1)S(1)}, u32[]{:S(2)}, u32[]{:S(2)}) collective-permute-start(bf16[192,256]{1,0:T(8,128)(2,1)S(1)} %get-tuple-element.103.mine), channel_id=1, source_target_pairs={{0,24},{1,9},{2,26},{3,11},{4,28},{5,13},{6,30},{7,15},{8,16},{9,1... | collective-permute-start | bytes 294920 | tf_op jit(solution)/shard_map/ppermute | solution.py:633
  69.6 3.5 %collective-permute-start.12 = (bf16[192,256]{1,0:T(8,128)(2,1)S(1)}, bf16[192,256]{1,0:T(8,128)(2,1)S(1)}, u32[]{:S(2)}, u32[]{:S(2)}) collective-permute-start(bf16[192,256]{1,0:T(8,128)(2,1)S(1)} %shard_map.344.mine), channel_id=1, source_target_pairs={{0,24},{1,9},{2,26},{3,11},{4,28},{5,13},{6,30},{7,15},{8,16},{9,1... | collective-permute-start | bytes 294920 | tf_op jit(solution)/shard_map/ppermute | solution.py:633
  69.7 5.4 %collective-permute-start.15 = (bf16[192,256]{1,0:T(8,128)(2,1)S(1)}, bf16[192,256]{1,0:T(8,128)(2,1)S(1)}, u32[]{:S(2)}, u32[]{:S(2)}) collective-permute-start(bf16[192,256]{1,0:T(8,128)(2,1)S(1)} %shard_map.346.mine), channel_id=1, source_target_pairs={{0,32},{1,97},{2,34},{3,99},{4,36},{5,101},{6,38},{7,103},{8,40},{... | collective-permute-start | bytes 294920 | tf_op jit(solution)/shard_map/ppermute | solution.py:633
  73.2 4.8 %collective-permute-start.13 = (bf16[192,256]{1,0:T(8,128)(2,1)S(1)}, bf16[192,256]{1,0:T(8,128)(2,1)S(1)}, u32[]{:S(2)}, u32[]{:S(2)}) collective-permute-start(bf16[192,256]{1,0:T(8,128)(2,1)S(1)} %shard_map.345.mine_a), channel_id=1, source_target_pairs={{0,32},{1,97},{2,34},{3,99},{4,36},{5,101},{6,38},{7,103},{8,40},{... | collective-permute-start | bytes 294920 | tf_op jit(solution)/shard_map/ppermute | solution.py:633
  75.1 3.5 %collective-permute-start.16 = (bf16[192,256]{1,0:T(8,128)(2,1)S(1)}, bf16[192,256]{1,0:T(8,128)(2,1)S(1)}, u32[]{:S(2)}, u32[]{:S(2)}) collective-permute-start(bf16[192,256]{1,0:T(8,128)(2,1)S(1)} %shard_map.347.mine_b), channel_id=1, source_target_pairs={{0,6},{1,3},{2,4},{3,1},{4,2},{5,7},{6,0},{7,5},{8,14},{9,11},{10,... | collective-permute-start | bytes 294920 | tf_op jit(solution)/shard_map/ppermute | solution.py:633
  78.7 21.9 %copy-start = (f32[256,1024]{1,0:T(8,128)S(1)}, f32[256,1024]{1,0:T(8,128)}, u32[]{:S(2)}) copy-start(f32[256,1024]{1,0:T(8,128)} %emb.5) | copy-start | bytes 3145732
  78.7 21.9 %copy-start.1 = (bf16[1024,256]{1,0:T(8,128)(2,1)S(1)}, bf16[1024,256]{1,0:T(8,128)(2,1)}, u32[]{:S(2)}) copy-start(bf16[1024,256]{1,0:T(8,128)(2,1)} %dense.5) | copy-start | bytes 1572868
  78.7 8.2 %collective-permute-start.23 = (bf16[384,256]{1,0:T(8,128)(2,1)S(1)}, bf16[384,256]{1,0:T(8,128)(2,1)S(1)}, u32[]{:S(2)}, u32[]{:S(2)}) collective-permute-start(bf16[384,256]{1,0:T(8,128)(2,1)S(1)} %shard_map.348.refs_0_), channel_id=1, source_target_pairs={{0,104},{1,57},{2,106},{3,59},{4,108},{5,61},{6,110},{7,63},{8,96}... | collective-permute-start | bytes 589832 | tf_op jit(solution)/shard_map/ppermute | solution.py:633
  79.5 9.4 %collective-permute-start.22 = (bf16[384,256]{1,0:T(8,128)(2,1)S(1)}, bf16[384,256]{1,0:T(8,128)(2,1)S(1)}, u32[]{:S(2)}, u32[]{:S(2)}) collective-permute-start(bf16[384,256]{1,0:T(8,128)(2,1)S(1)} %shard_map.348.refs_0_), channel_id=1, source_target_pairs={{0,98},{1,39},{2,96},{3,37},{4,102},{5,35},{6,100},{7,33},{8,106},... | collective-permute-start | bytes 589832 | tf_op jit(solution)/shard_map/ppermute | solution.py:633
  81.0 10.0 %collective-permute-start.21 = (bf16[384,256]{1,0:T(8,128)(2,1)S(1)}, bf16[384,256]{1,0:T(8,128)(2,1)S(1)}, u32[]{:S(2)}, u32[]{:S(2)}) collective-permute-start(bf16[384,256]{1,0:T(8,128)(2,1)S(1)} %shard_map.348.refs_0_), channel_id=1, source_target_pairs={{0,10},{1,31},{2,8},{3,29},{4,14},{5,27},{6,12},{7,25},{8,2},{9,23... | collective-permute-start | bytes 589832 | tf_op jit(solution)/shard_map/ppermute | solution.py:633
  84.8 8.9 %collective-permute-start.20 = (bf16[384,256]{1,0:T(8,128)(2,1)S(1)}, bf16[384,256]{1,0:T(8,128)(2,1)S(1)}, u32[]{:S(2)}, u32[]{:S(2)}) collective-permute-start(bf16[384,256]{1,0:T(8,128)(2,1)S(1)} %shard_map.348.refs_0_), channel_id=1, source_target_pairs={{0,106},{1,63},{2,104},{3,61},{4,110},{5,59},{6,108},{7,57},{8,98}... | collective-permute-start | bytes 589832 | tf_op jit(solution)/shard_map/ppermute | solution.py:633
  86.1 7.7 %collective-permute-start.19 = (bf16[384,256]{1,0:T(8,128)(2,1)S(1)}, bf16[384,256]{1,0:T(8,128)(2,1)S(1)}, u32[]{:S(2)}, u32[]{:S(2)}) collective-permute-start(bf16[384,256]{1,0:T(8,128)(2,1)S(1)} %shard_map.348.refs_0_), channel_id=1, source_target_pairs={{0,96},{1,33},{2,98},{3,35},{4,100},{5,37},{6,102},{7,39},{8,104},... | collective-permute-start | bytes 589832 | tf_op jit(solution)/shard_map/ppermute | solution.py:633
  87.0 6.8 %collective-permute-start.18 = (bf16[384,256]{1,0:T(8,128)(2,1)S(1)}, bf16[384,256]{1,0:T(8,128)(2,1)S(1)}, u32[]{:S(2)}, u32[]{:S(2)}) collective-permute-start(bf16[384,256]{1,0:T(8,128)(2,1)S(1)} %shard_map.348.refs_0_), channel_id=1, source_target_pairs={{0,8},{1,25},{2,10},{3,27},{4,12},{5,29},{6,14},{7,31},{8,0},{9,17... | collective-permute-start | bytes 589832 | tf_op jit(solution)/shard_map/ppermute | solution.py:633
  88.9 7.1 %collective-permute-start.17 = (bf16[384,256]{1,0:T(8,128)(2,1)S(1)}, bf16[384,256]{1,0:T(8,128)(2,1)S(1)}, u32[]{:S(2)}, u32[]{:S(2)}) collective-permute-start(bf16[384,256]{1,0:T(8,128)(2,1)S(1)} %shard_map.348.refs_0_), channel_id=1, source_target_pairs={{0,2},{1,7},{2,0},{3,5},{4,6},{5,3},{6,4},{7,1},{8,10},{9,15},{10,... | collective-permute-start | bytes 589832 | tf_op jit(solution)/shard_map/ppermute | solution.py:633
  96.1 7.6 %collective-permute-start.24 = (bf16[3072,256]{1,0:T(8,128)(2,1)S(1)}, bf16[3072,256]{1,0:T(8,128)(2,1)S(1)}, u32[]{:S(2)}, u32[]{:S(2)}) collective-permute-start(bf16[3072,256]{1,0:T(8,128)(2,1)S(1)} %shard_map.349.mine), channel_id=1, source_target_pairs={{0,1},{1,0},{2,3},{3,2},{4,5},{5,4},{6,7},{7,6},{8,9},{9,8},{10,11... | collective-permute-start | bytes 4718600 | tf_op jit(solution)/shard_map/ppermute | solution.py:516
